TPU v7x, 32 devices: a whole 2x2x4 slice. The times are simulated.
32 devices in a mesh: seq: 8 (over z, y), fsdp: 4 (over x, core).
Axes of the slice: x: 2, y: 2, z: 4, core: 2. Of those that a mesh axis runs over, the one named last changes fastest.
Arguments:
- tokens_in: bfloat16 [2, 2048, 2048], P(None, 'seq', 'fsdp'), may hold values from -6 to 6
- cotangent: bfloat16 [2, 2048, 2048], P(None, 'seq', 'fsdp'), may hold values from -6 to 6
- gain_attn: bfloat16 [2048], P('seq'), may hold values from 0.099609375 to 1.8984375
- query_weight: bfloat16 [2048, 2048], P('seq', 'fsdp'), may hold values from -0.0625 to 0.0625
- key_weight: bfloat16 [2048, 2048], P('seq', 'fsdp'), may hold values from -0.0625 to 0.0625
- value_weight: bfloat16 [2048, 2048], P('seq', 'fsdp'), may hold values from -0.125 to 0.125
- output_weight: bfloat16 [2048, 2048], P('seq', 'fsdp'), may hold values from -0.75 to 0.75
- bias_table: bfloat16 [32, 32], P('seq', 'fsdp'), may hold values from -6 to 6
- gain_ffn: bfloat16 [2048], P('seq'), may hold values from 0.099609375 to 1.8984375
- gate_weight: bfloat16 [2048, 5120], P('seq', 'fsdp'), may hold values from -0.125 to 0.125
- up_weight: bfloat16 [2048, 5120], P('seq', 'fsdp'), may hold values from -0.125 to 0.125
- down_weight: bfloat16 [2048, 5120], P('seq', 'fsdp'), may hold values from -0.078125 to 0.078125
- lengths: int32 [2], replicated, may hold values from 256 to 2048, as said below
- buckets: int32 [4095], replicated, may hold values from 0 to 31
Outputs:
- layer_out: bfloat16 [2, 2048, 2048], P(None, 'seq', 'fsdp')
- grad_tokens: float32 [2, 2048, 2048], P(None, 'seq', 'fsdp')
- grad_gain_attn: float32 [2048], P('seq')
- grad_query: float32 [2048, 2048], P('seq', 'fsdp')
- grad_key: float32 [2048, 2048], P('seq', 'fsdp')
- grad_value: float32 [2048, 2048], P('seq', 'fsdp')
- grad_output: float32 [2048, 2048], P('seq', 'fsdp')
- grad_table: float32 [32, 32], P('seq', 'fsdp')
- grad_gain_ffn: float32 [2048], P('seq')
- grad_gate: float32 [2048, 5120], P('seq', 'fsdp')
- grad_up: float32 [2048, 5120], P('seq', 'fsdp')
- grad_down: float32 [2048, 5120], P('seq', 'fsdp')
Inputs may be any that keep to these rules, and one draw needn't show every extreme that they name: `lengths`: exactly one of the 2 sequences is valid over all 2048 slots; the others end at least 256 slots earlier.
All inputs are finite; a program needn't handle non-finite values.
Results may differ from a plain program's by a relative error of at most 0.014.
The roundings to bfloat16 on the way count: a program that leaves them out, or rounds other values in their place, can miss the bound.
Values may be sent and summed in bfloat16 or wider, within the bound.
A program may use at most 384 MiB of HBM per device.

v0:
```python
from functools import partial

import jax
import jax.numpy as jnp
from jax import lax
from jax.experimental import pallas as pl
from jax.experimental.pallas import tpu as pltpu
from jax.sharding import PartitionSpec as P

DH = 64


epsilon = 1e-06
highest = lax.Precision.HIGHEST
masked_score = -1e30


def plain_product(left, right):
    return jnp.dot(left, right, preferred_element_type=jnp.float32)


def right_transposed(left, right):
    return lax.dot_general(
        left, right, (((1,), (1,)), ((), ())), preferred_element_type=jnp.float32
    )


def left_transposed(left, right):
    return lax.dot_general(
        left, right, (((0,), (0,)), ((), ())), preferred_element_type=jnp.float32
    )


def normalize(rows, gain):
    row_scale = lax.rsqrt(jnp.mean(rows * rows, axis=-1, keepdims=True) + epsilon)
    unit_rows = rows * row_scale
    return (unit_rows, row_scale, (unit_rows * gain.astype(jnp.float32)).astype(jnp.bfloat16))


def norm_back(grad_normed, unit_rows, row_scale, gain):
    weighted = grad_normed * gain.astype(jnp.float32)
    return row_scale * (
        weighted - unit_rows * jnp.mean(weighted * unit_rows, axis=-1, keepdims=True)
    )


def to_heads(rows, batch_count, head_size):
    slot_count = rows.shape[0] // batch_count
    number_of_heads = rows.shape[1] // head_size
    return rows.reshape(batch_count, slot_count, number_of_heads, head_size).transpose(2, 0, 1, 3)


def from_heads(blocks):
    number_of_heads, batch_count, slot_count, head_size = blocks.shape
    return blocks.transpose(1, 2, 0, 3).reshape(
        batch_count * slot_count, number_of_heads * head_size
    )


def bias_rows(bias_line, first_query, slot_count, length):
    span = slot_count + length - 1
    segment = lax.dynamic_slice_in_dim(bias_line, length - first_query - slot_count, span)
    flat = jnp.tile(segment, slot_count)
    skewed = flat[slot_count - 1 : slot_count - 1 + slot_count * (span - 1)].reshape(
        slot_count, span - 1
    )
    return skewed[:, :length]


def bias_rows_back(block_grad, first_query, slot_count, length, line_length):
    span = slot_count + length - 1
    widened = jnp.pad(block_grad, ((0, 0), (0, span - 1 - length)))
    flat = jnp.pad(widened.reshape(-1), (slot_count - 1, 1))
    segment_grad = jnp.sum(flat.reshape(slot_count, span), axis=0)
    return lax.dynamic_update_slice_in_dim(
        jnp.zeros((line_length,), jnp.float32), segment_grad, length - first_query - slot_count, 0
    )


def full_features(block):
    gathered = lax.all_gather(block, "fsdp", axis=2, tiled=True)
    return gathered.reshape(gathered.shape[0] * gathered.shape[1], gathered.shape[2])


def feature_total(partial_rows):
    return lax.psum(partial_rows, "fsdp")


def shards(
    tokens_in,
    cotangent,
    gain_attn,
    query_weight,
    key_weight,
    value_weight,
    output_weight,
    bias_table,
    gain_ffn,
    gate_weight,
    up_weight,
    down_weight,
    lengths,
    buckets,
):
    batch_count, slot_count, part_width = tokens_in.shape
    head_size = DH
    seq_index = lax.axis_index("seq")
    fsdp_index = lax.axis_index("fsdp")
    length = slot_count * lax.axis_size("seq")
    line_length = buckets.shape[0]
    first_query = seq_index * slot_count
    positions = jnp.arange(length, dtype=jnp.int32)
    query_positions = first_query + jnp.arange(slot_count, dtype=jnp.int32)
    key_valid = positions[None, :] < lengths[:, None]
    own_valid = query_positions[None, :] < lengths[:, None]
    gain_one, query_full, key_full, value_full, output_full, table_full = (
        lax.all_gather(gain_attn, "seq", axis=0, tiled=True),
        lax.all_gather(query_weight, "seq", axis=0, tiled=True),
        lax.all_gather(key_weight, "seq", axis=0, tiled=True),
        lax.all_gather(value_weight, "seq", axis=0, tiled=True),
        lax.all_gather(output_weight, "seq", axis=0, tiled=True),
        lax.all_gather(bias_table, "seq", axis=0, tiled=True),
    )
    token_rows = full_features(tokens_in).astype(jnp.float32)
    unit_one, scale_one, normed_one = normalize(token_rows, gain_one)
    query_heads = to_heads(
        plain_product(normed_one, query_full).astype(jnp.bfloat16), batch_count, head_size
    )
    key_heads = to_heads(
        plain_product(normed_one, key_full).astype(jnp.bfloat16), batch_count, head_size
    )
    value_heads = to_heads(
        plain_product(normed_one, value_full).astype(jnp.bfloat16), batch_count, head_size
    )
    number_of_heads = query_heads.shape[0]
    flat_shape = (number_of_heads, batch_count, slot_count * head_size)
    gathered_keys, gathered_values = (
        lax.all_gather(key_heads.reshape(flat_shape), "seq", axis=2, tiled=True),
        lax.all_gather(value_heads.reshape(flat_shape), "seq", axis=2, tiled=True),
    )
    all_keys = gathered_keys.reshape(number_of_heads, batch_count, length, head_size)
    all_values = gathered_values.reshape(number_of_heads, batch_count, length, head_size)
    bucket_hot = (
        buckets[:, None] == jnp.arange(table_full.shape[0], dtype=jnp.int32)[None, :]
    ).astype(jnp.float32)
    offset_bias = lax.dot_general(
        table_full.astype(jnp.float32), bucket_hot, (((0,), (1,)), ((), ())), precision=highest
    )

    def masked_scores(query_tile_rows, key_tile_rows, bias_block):
        raw = (
            jnp.einsum(
                "jht,jxt->jhx", query_tile_rows, key_tile_rows, preferred_element_type=jnp.float32
            )
            + bias_block[None]
        )
        return jnp.where(key_valid[:, None, :], raw, masked_score)

    def attend(inputs):
        query_tile_rows, key_tile_rows, value_tile_rows, bias_line = inputs
        scores = masked_scores(
            query_tile_rows, key_tile_rows, bias_rows(bias_line, first_query, slot_count, length)
        )
        row_peak = jnp.max(scores, axis=-1, keepdims=True)
        raised = jnp.exp(scores - row_peak)
        denominator = jnp.sum(raised, axis=-1, keepdims=True)
        weights_reduced_precision = (raised / denominator).astype(jnp.bfloat16)
        context = jnp.einsum(
            "wot,wtf->wof",
            weights_reduced_precision,
            value_tile_rows,
            preferred_element_type=jnp.float32,
        ).astype(jnp.bfloat16)
        return (context, (row_peak + jnp.log(denominator))[..., 0])

    context_heads, log_totals = lax.map(attend, (query_heads, all_keys, all_values, offset_bias))
    context_rows = from_heads(context_heads)
    residual = token_rows + feature_total(right_transposed(context_rows, output_full))
    gain_two, gate_full, up_full, down_full = (
        lax.all_gather(gain_ffn, "seq", axis=0, tiled=True),
        lax.all_gather(gate_weight, "seq", axis=0, tiled=True),
        lax.all_gather(up_weight, "seq", axis=0, tiled=True),
        lax.all_gather(down_weight, "seq", axis=0, tiled=True),
    )
    unit_two, scale_two, normed_two = normalize(residual, gain_two)
    gate_pre = plain_product(normed_two, gate_full)
    up_pre = plain_product(normed_two, up_full)
    activated, gelu_back = jax.vjp(jax.nn.gelu, gate_pre)
    hidden = (activated * up_pre).astype(jnp.bfloat16)
    ffn_share = lax.psum_scatter(
        right_transposed(hidden, down_full), "fsdp", scatter_dimension=1, tiled=True
    )
    residual_share = lax.dynamic_slice_in_dim(residual, fsdp_index * part_width, part_width, 1)
    layer_out = (
        (residual_share + ffn_share)
        .astype(jnp.bfloat16)
        .reshape(batch_count, slot_count, part_width)
    )
    masked_cot = jnp.where(own_valid[:, :, None], cotangent, jnp.zeros_like(cotangent))
    grad_rows = full_features(masked_cot)
    grad_down = left_transposed(grad_rows, hidden)
    grad_hidden = plain_product(grad_rows, down_full)
    grad_gate_pre = gelu_back(grad_hidden * up_pre)[0].astype(jnp.bfloat16)
    grad_up_pre = (grad_hidden * activated).astype(jnp.bfloat16)
    grad_gate = left_transposed(normed_two, grad_gate_pre)
    grad_up = left_transposed(normed_two, grad_up_pre)
    normed_two_grad = right_transposed(grad_gate_pre, gate_full) + right_transposed(
        grad_up_pre, up_full
    )
    second_gain_piece = jnp.sum(normed_two_grad * unit_two, axis=0)
    ffn_grads = (
        lax.psum_scatter(second_gain_piece, "seq", scatter_dimension=0, tiled=True),
        lax.psum_scatter(grad_gate, "seq", scatter_dimension=0, tiled=True),
        lax.psum_scatter(grad_up, "seq", scatter_dimension=0, tiled=True),
        lax.psum_scatter(grad_down, "seq", scatter_dimension=0, tiled=True),
    )
    residual_grad = grad_rows.astype(jnp.float32) + norm_back(
        feature_total(normed_two_grad), unit_two, scale_two, gain_two
    )
    residual_low = residual_grad.astype(jnp.bfloat16)
    grad_output = left_transposed(residual_low, context_rows)
    context_grad = to_heads(
        plain_product(residual_low, output_full).astype(jnp.bfloat16), batch_count, head_size
    )

    def query_side(inputs, with_keys):
        query_tile_rows, key_tile_rows, value_tile_rows, bias_line, log_total, context_tile_rows = (
            inputs
        )
        scores = masked_scores(
            query_tile_rows, key_tile_rows, bias_rows(bias_line, first_query, slot_count, length)
        )
        probs = jnp.exp(scores - log_total[..., None])
        prob_grad = jnp.einsum(
            "jht,jxt->jhx", context_tile_rows, value_tile_rows, preferred_element_type=jnp.float32
        )
        delta = jnp.sum(probs * prob_grad, axis=-1)
        score_gradient = (probs * (prob_grad - delta[..., None])).astype(jnp.bfloat16)
        query_grad = jnp.einsum(
            "wot,wtf->wof", score_gradient, key_tile_rows, preferred_element_type=jnp.float32
        )
        bias_grad = bias_rows_back(
            jnp.sum(score_gradient.astype(jnp.float32), axis=0),
            first_query,
            slot_count,
            length,
            line_length,
        )
        key_term = jnp.einsum(
            "xic,xil->xcl", score_gradient, query_tile_rows, preferred_element_type=jnp.float32
        )
        value_term = jnp.einsum(
            "xic,xil->xcl",
            probs.astype(jnp.bfloat16),
            context_tile_rows,
            preferred_element_type=jnp.float32,
        )
        return (query_grad, bias_grad, delta, key_term, value_term)

    side_inputs = (query_heads, all_keys, all_values, offset_bias, log_totals, context_grad)
    query_grad, bias_grad, delta, key_terms, value_terms = lax.map(
        partial(query_side, with_keys=True), side_inputs
    )
    wide_shape = (number_of_heads, batch_count, length * head_size)
    key_sums, value_sums = (
        lax.psum_scatter(key_terms.reshape(wide_shape), "seq", scatter_dimension=2, tiled=True),
        lax.psum_scatter(value_terms.reshape(wide_shape), "seq", scatter_dimension=2, tiled=True),
    )
    own_shape = (number_of_heads, batch_count, slot_count, head_size)
    query_low = from_heads(query_grad.astype(jnp.bfloat16))
    key_low = from_heads(key_sums.reshape(own_shape).astype(jnp.bfloat16))
    value_low = from_heads(value_sums.reshape(own_shape).astype(jnp.bfloat16))
    grad_query = left_transposed(normed_one, query_low)
    grad_key = left_transposed(normed_one, key_low)
    grad_value = left_transposed(normed_one, value_low)
    grad_table = lax.dot_general(bucket_hot, bias_grad, (((0,), (1,)), ((), ())), precision=highest)
    normed_one_grad = (
        right_transposed(query_low, query_full)
        + right_transposed(key_low, key_full)
        + right_transposed(value_low, value_full)
    )
    gain_one_part = jnp.sum(normed_one_grad * unit_one, axis=0)
    attn_grads = (
        lax.psum_scatter(gain_one_part, "seq", scatter_dimension=0, tiled=True),
        lax.psum_scatter(grad_query, "seq", scatter_dimension=0, tiled=True),
        lax.psum_scatter(grad_key, "seq", scatter_dimension=0, tiled=True),
        lax.psum_scatter(grad_value, "seq", scatter_dimension=0, tiled=True),
        lax.psum_scatter(grad_output, "seq", scatter_dimension=0, tiled=True),
        lax.psum_scatter(grad_table, "seq", scatter_dimension=0, tiled=True),
    )
    token_grad = residual_grad + norm_back(
        feature_total(normed_one_grad), unit_one, scale_one, gain_one
    )
    token_share = lax.dynamic_slice_in_dim(
        token_grad, fsdp_index * part_width, part_width, 1
    ).reshape(batch_count, slot_count, part_width)
    gain_one_sum, gain_two_sum = lax.psum((attn_grads[0], ffn_grads[0]), "fsdp")
    return (
        layer_out,
        token_share,
        gain_one_sum,
        attn_grads[1],
        attn_grads[2],
        attn_grads[3],
        attn_grads[4],
        attn_grads[5],
        gain_two_sum,
        ffn_grads[1],
        ffn_grads[2],
        ffn_grads[3],
    )


BLOCK = 128
BOTH = ("seq", "fsdp")


def move(value, target):
    pairs = []
    for z in range(4):
        for y in range(2):
            for x in range(2):
                for c in range(2):
                    zt, yt, xt, ct = target(z, y, x, c)
                    pairs.append(((2 * z + y) * 4 + 2 * x + c, (2 * zt + yt) * 4 + 2 * xt + ct))
    return lax.ppermute(value, BOTH, pairs)


def spread_slot(k):
    return lambda z, y, x, c: (2 * c + (k ^ (z & 1)), y, x, z >> 1)


def spread_plane(dy, dx):
    return lambda z, y, x, c: (z, y ^ dy, c ^ dx, x)


def join_plane(dy, dx):
    return lambda z, y, x, c: (z, y ^ dy, c, x ^ dx)


def along_z(d):
    return lambda z, y, x, c: (z ^ d, y, x, c)


def other_core(z, y, x, c):
    return (z, y, x, c ^ 1)


def across(dx, dy):
    return lambda z, y, x, c: (z, y ^ dy, x ^ dx, c)


def across_fsdp(d):
    return lambda z, y, x, c: (z, y, x ^ (d >> 1), c ^ (d & 1))


def in_place(relative, me):
    current, bit = list(relative), 1
    while bit < len(current):
        swap = (me & bit) != 0
        current = [jnp.where(swap, current[i ^ bit], current[i]) for i in range(len(current))]
        bit *= 2
    return current


def sum_rows(mine, other):
    mine = mine + move(other, other_core).astype(jnp.float32)
    count = mine.shape[0] // 4
    total = mine[:count]
    for d in (1, 2, 3):
        part = mine[d * count : (d + 1) * count].astype(jnp.bfloat16)
        total = total + move(part, along_z(d)).astype(jnp.float32)
    return total


KEYS = 256
QUERIES = 256
OFFSET = 1920


def skew_table(rev_ref, table):
    width = rev_ref.shape[1]
    line = jnp.broadcast_to(rev_ref[...], (8, width))
    for first in range(0, BLOCK, 8):
        table[first : first + 8, :] = pltpu.roll(
            line, (width - (BLOCK - 1) + first) % width, axis=1, stride=1, stride_axis=0
        )


def place_of(piece, part, z, y, x, c):
    c_rel, d = part // 4, part % 4
    b = jnp.bitwise_xor(x, piece // 2)
    block = (
        4 * jnp.bitwise_xor(z, d)
        + 2 * jnp.bitwise_xor(y, piece % 2)
        + jnp.bitwise_xor(c, c_rel)
    )
    return b, block


def part_of(b, block, z, y, x, c):
    piece = 2 * jnp.bitwise_xor(b, x) + jnp.bitwise_xor((block // 2) % 2, y)
    part = 4 * jnp.bitwise_xor(block % 2, c) + jnp.bitwise_xor(block // 4, z)
    return piece, part


def lanes(first, count):
    return pl.ds(pl.multiple_of(first, BLOCK), count)


def attend_kernel(sc, pieces, rev_ref, ctx_ref, ctx_wide, lse_ref, qkv, keys, table):
    z, y, x, c = position()
    for piece in range(4):
        for part in range(8):
            b, block = place_of(piece, part, z, y, x, c)
            data = pieces[piece, :, :, part * BLOCK : (part + 1) * BLOCK]
            qkv[b, :, :, lanes(block * BLOCK, BLOCK)] = data
            keys[b, lanes(block * BLOCK, BLOCK), :] = data[1].T
    skew_table(rev_ref, table)
    length = qkv.shape[-1]
    for b in range(2):
        valid = sc[b]
        full = valid // KEYS

        @pl.loop(0, length // QUERIES)
        def _(i):
            first_query = i * QUERIES
            query = qkv[b, 0, :, lanes(first_query, QUERIES)]

            def tile(j, carry, masked):
                peak, total, acc = carry
                first_key = j * KEYS
                score = jnp.dot(
                    keys[b, lanes(first_key, KEYS), :], query, preferred_element_type=jnp.float32
                )
                score = score + jnp.concatenate(
                    [
                        table[:, lanes(first_query - first_key + OFFSET - t, QUERIES)]
                        for t in range(0, KEYS, BLOCK)
                    ],
                    axis=0,
                )
                if masked:
                    position = first_key + lax.broadcasted_iota(jnp.int32, (KEYS, QUERIES), 0)
                    score = jnp.where(position < valid, score, masked_score)
                now = jnp.maximum(peak, jnp.max(score, axis=0, keepdims=True))
                scale = jnp.exp(peak - now)
                prob = jnp.exp(score - now)
                total = total * scale + jnp.sum(prob, axis=0, keepdims=True)
                acc = acc * scale + jnp.dot(
                    qkv[b, 2, :, lanes(first_key, KEYS)],
                    prob.astype(jnp.bfloat16),
                    preferred_element_type=jnp.float32,
                )
                return now, total, acc

            carry = (
                jnp.full((1, QUERIES), masked_score, jnp.float32),
                jnp.zeros((1, QUERIES), jnp.float32),
                jnp.zeros((DH, QUERIES), jnp.float32),
            )
            carry = lax.fori_loop(0, full, lambda j, s: tile(j, s, False), carry)
            peak, total, acc = lax.cond(
                valid > full * KEYS, lambda s: tile(full, s, True), lambda s: s, carry
            )
            context = acc / total
            ctx_wide[b, :, lanes(first_query, QUERIES)] = context
            lse_ref[b, :, lanes(first_query, QUERIES)] = peak + jnp.log(total)
            low = context.astype(jnp.bfloat16)
            for t in range(QUERIES // BLOCK):
                piece, part = part_of(b, i * (QUERIES // BLOCK) + t, z, y, x, c)
                ctx_ref[piece, :, lanes(part * BLOCK, BLOCK)] = low[:, t * BLOCK : (t + 1) * BLOCK]


def attend(scalars, pieces, rev_line):
    _, _, head_size, tokens = pieces.shape
    length = tokens * 2
    smem, vmem = pl.BlockSpec(memory_space=pltpu.SMEM), pl.BlockSpec(memory_space=pltpu.VMEM)
    return pl.pallas_call(
        attend_kernel,
        name="attend",
        out_shape=[
            jax.ShapeDtypeStruct((4, head_size, tokens), jnp.bfloat16),
            jax.ShapeDtypeStruct((2, head_size, length), jnp.float32),
            jax.ShapeDtypeStruct((2, 1, length), jnp.float32),
            jax.ShapeDtypeStruct((2, 3, head_size, length), jnp.bfloat16),
        ],
        in_specs=[smem] + [vmem] * 2,
        out_specs=[vmem] * 4,
        scratch_shapes=[
            pltpu.VMEM((2, length, head_size), jnp.bfloat16),
            pltpu.VMEM((BLOCK, rev_line.shape[1]), jnp.float32),
        ],
        cost_estimate=pl.CostEstimate(
            flops=46_000_000_000, bytes_accessed=4 << 20, transcendentals=0
        ),
        compiler_params=pltpu.CompilerParams(vmem_limit_bytes=48 << 20),
    )(scalars, pieces, rev_line)


def attend_back_kernel(
    sc, pieces, rev_ref, ctx_wide, lse_ref, qkv,
    out_ref, line_ref,
    queries, keys, values, grads, grads_t, delta, query_sum, key_sum, value_sum, table, table_sum,
):
    z, y, x, c = position()
    length = qkv.shape[-1]
    for piece in range(4):
        for part in range(8):
            b, block = place_of(piece, part, z, y, x, c)
            data = pieces[piece, :, part * BLOCK : (part + 1) * BLOCK]
            grads_t[b, :, lanes(block * BLOCK, BLOCK)] = data
            grads[b, lanes(block * BLOCK, BLOCK), :] = data.T
    for b in range(2):
        for first in range(0, length, BLOCK):
            here = slice(first, first + BLOCK)
            queries[b, here, :] = qkv[b, 0, :, here].T
            keys[b, here, :] = qkv[b, 1, :, here].T
            values[b, here, :] = qkv[b, 2, :, here].T
        delta[b] = jnp.sum(
            ctx_wide[b] * grads_t[b].astype(jnp.float32), axis=0, keepdims=True
        )
    skew_table(rev_ref, table)
    table_sum[...] = jnp.zeros_like(table_sum)
    query_sum[...] = jnp.zeros_like(query_sum)
    out_ref[...] = jnp.zeros_like(out_ref)
    for b in range(2):
        valid = sc[b]
        full = valid // KEYS
        count = (valid + KEYS - 1) // KEYS

        def key_step(j, masked):
            first_key = j * KEYS
            key, value = keys[b, lanes(first_key, KEYS), :], values[b, lanes(first_key, KEYS), :]
            key_t = qkv[b, 1, :, lanes(first_key, KEYS)]
            key_sum[...] = jnp.zeros_like(key_sum)
            value_sum[...] = jnp.zeros_like(value_sum)

            @pl.loop(0, count)
            def _(i):
                first_query = i * QUERIES
                here = lanes(first_query, QUERIES)
                score = jnp.dot(key, qkv[b, 0, :, here], preferred_element_type=jnp.float32)
                score = score + jnp.concatenate(
                    [
                        table[:, lanes(first_query - first_key + OFFSET - t, QUERIES)]
                        for t in range(0, KEYS, BLOCK)
                    ],
                    axis=0,
                )
                if masked:
                    position = first_key + lax.broadcasted_iota(jnp.int32, (KEYS, QUERIES), 0)
                    score = jnp.where(position < valid, score, masked_score)
                prob = jnp.exp(score - lse_ref[b, :, here])
                prob_grad = jnp.dot(value, grads_t[b, :, here], preferred_element_type=jnp.float32)
                score_grad = (prob * (prob_grad - delta[b, :, here])).astype(jnp.bfloat16)
                value_sum[...] += jnp.dot(
                    prob.astype(jnp.bfloat16), grads[b, here, :], preferred_element_type=jnp.float32
                )
                key_sum[...] += jnp.dot(
                    score_grad, queries[b, here, :], preferred_element_type=jnp.float32
                )
                query_sum[b, :, here] += jnp.dot(
                    key_t, score_grad, preferred_element_type=jnp.float32
                )
                for t in range(0, KEYS, BLOCK):
                    table_sum[:, lanes(first_query - first_key + OFFSET - t, QUERIES)] += score_grad[
                        t : t + BLOCK
                    ].astype(jnp.float32)

            for t in range(KEYS // BLOCK):
                piece, part = part_of(b, j * (KEYS // BLOCK) + t, z, y, x, c)
                rows = slice(t * BLOCK, (t + 1) * BLOCK)
                at = lanes(part * BLOCK, BLOCK)
                out_ref[piece, 1, :, at] = key_sum[rows, :].T.astype(jnp.bfloat16)
                out_ref[piece, 2, :, at] = value_sum[rows, :].T.astype(jnp.bfloat16)

        pl.loop(0, full)(lambda j: key_step(j, False))
        pl.when(valid > full * KEYS)(lambda: key_step(full, True))
        for block in range(length // BLOCK):
            piece, part = part_of(b, block, z, y, x, c)
            out_ref[piece, 0, :, lanes(part * BLOCK, BLOCK)] = query_sum[
                b, :, block * BLOCK : (block + 1) * BLOCK
            ].astype(jnp.bfloat16)
    width = table_sum.shape[1]
    line = jnp.zeros((8, width), jnp.float32)
    for first in range(0, BLOCK, 8):
        line = line + pltpu.roll(table_sum[first : first + 8, :], BLOCK - 8 - first, axis=1)
    ahead = 7 - lax.broadcasted_iota(jnp.int32, (8, width), 0)
    for bit in (1, 2, 4):
        line = jnp.where((ahead & bit) != 0, pltpu.roll(line, bit, axis=1), line)
    line_ref[...] = jnp.sum(line, axis=0, keepdims=True)


def attend_back(scalars, pieces, rev_line, ctx_wide, lse, qkv):
    _, head_size, tokens = pieces.shape
    length = tokens * 2
    smem, vmem = pl.BlockSpec(memory_space=pltpu.SMEM), pl.BlockSpec(memory_space=pltpu.VMEM)
    low = pltpu.VMEM((2, length, head_size), jnp.bfloat16)
    return pl.pallas_call(
        attend_back_kernel,
        name="attend_back",
        out_shape=[
            jax.ShapeDtypeStruct((4, 3, head_size, tokens), jnp.bfloat16),
            jax.ShapeDtypeStruct(rev_line.shape, jnp.float32),
        ],
        in_specs=[smem] + [vmem] * 5,
        out_specs=[vmem] * 2,
        scratch_shapes=[
            low, low, low, low,
            pltpu.VMEM((2, head_size, length), jnp.bfloat16),
            pltpu.VMEM((2, 1, length), jnp.float32),
            pltpu.VMEM((2, head_size, length), jnp.float32),
            pltpu.VMEM((KEYS, head_size), jnp.float32),
            pltpu.VMEM((KEYS, head_size), jnp.float32),
            pltpu.VMEM((BLOCK, rev_line.shape[1]), jnp.float32),
            pltpu.VMEM((BLOCK, rev_line.shape[1]), jnp.float32),
        ],
        cost_estimate=pl.CostEstimate(
            flops=46_000_000_000, bytes_accessed=4 << 20, transcendentals=0
        ),
        compiler_params=pltpu.CompilerParams(vmem_limit_bytes=48 << 20),
    )(scalars, pieces, rev_line, ctx_wide, lse, qkv)


CHUNKS = 2
MESH_ID = pl.DeviceIdType.MESH
IN_VMEM = pl.BlockSpec(memory_space=pltpu.VMEM)
IN_PLACE = pl.BlockSpec(memory_space=pl.ANY)
COPIES = pltpu.SemaphoreType.DMA


def flip(a, b):
    return a + b - 2 * a * b


def flip_pair(a, b):
    return 2 * flip(a // 2, b // 2) + flip(a % 2, b % 2)


def position():
    s, f = lax.axis_index("seq"), lax.axis_index("fsdp")
    return s // 2, s % 2, f // 2, f % 2


def device(z, y, x, c):
    return (2 * z + y, 2 * x + c)


def ring_of(z):
    high, low = z // 2, z % 2
    following = 2 * low + 1 - high
    return following, (2 * (1 - low) + high, 2 * (1 - high) + 1 - low, following)


def greet(z, y, x, c):
    peers = []
    for d in range(1, 8):
        peers.append(device(z, flip(y, d // 4), flip(x, (d // 2) % 2), flip(c, d % 2)))
        if d > 1:
            peers.append(device(flip_pair(z, d // 2), y, x, flip(c, d % 2)))
    barrier = pltpu.get_barrier_semaphore()
    for peer in peers:
        pl.semaphore_signal(barrier, inc=1, device_id=peer, device_id_type=MESH_ID)
    pl.semaphore_wait(barrier, len(peers))


def remote(source, target, send, recv, to):
    return pltpu.make_async_remote_copy(
        src_ref=source,
        dst_ref=target,
        send_sem=send,
        recv_sem=recv,
        device_id=to,
        device_id_type=MESH_ID,
    )


class Links:
    def __init__(self, send, recv):
        self.send, self.recv, self.used, self.sent = send, recv, 0, []

    def go(self, source, target, to):
        i = self.used
        self.used += 1
        made = remote(source, target, self.send.at[i], self.recv.at[i], to)
        made.start()
        self.sent.append(made)
        return made

    def go_unless(self, own, source, target, to, send=None, recv=None):
        if send is None:
            send, recv = self.send.at[self.used], self.recv.at[self.used]
            self.used += 1
        made = remote(source, target, send, recv, to)
        if own is None:
            made.start()
            self.sent.append(made)
            return made
        local = pltpu.make_async_copy(source, target, recv)
        pl.when(own)(lambda: local.start())
        pl.when(jnp.logical_not(own))(lambda: made.start())
        self.sent.append((own, made))
        return made

    def done(self, made):
        made.wait_send()
        self.sent = [m for m in self.sent if m is not made]

    def finish(self):
        for made in self.sent:
            if isinstance(made, tuple):
                pl.when(jnp.logical_not(made[0]))(lambda made=made: made[1].wait_send())
            else:
                made.wait_send()


def share_start(links, rows_all, me):
    z, y, x, c = me
    following, _ = ring_of(z)
    rows = rows_all.shape[1] // CHUNKS
    ring = []
    for h in range(CHUNKS):
        here = pl.ds(h * rows, rows)
        target = rows_all.at[flip_pair(following, z), here]
        ring.append(links.go(rows_all.at[0, here], target, device(following, y, x, c)))
    core = [links.go(rows_all.at[0], rows_all.at[4], device(z, y, x, 1 - c))]
    return [ring], core


def share_step(links, rows_all, me, state, step):
    z, y, x, c = me
    following, back = ring_of(z)
    rows = rows_all.shape[1] // CHUNKS
    ring, core = state
    slot = flip_pair(z, back[step - 1])
    sent = []
    for h in range(CHUNKS):
        here = pl.ds(h * rows, rows)
        ring[-1][h].wait_recv()
        source = rows_all.at[slot, here]
        if step < 3:
            target = rows_all.at[flip_pair(following, back[step - 1]), here]
            sent.append(links.go(source, target, device(following, y, x, c)))
        core.append(links.go(source, rows_all.at[4 + slot, here], device(z, y, x, 1 - c)))
    ring.append(sent)


def share_end(state):
    for made in state[1]:
        made.wait_recv()


def sum_order(z):
    _, back = ring_of(z)
    return [flip_pair(z, b) for b in back] + [0]


def reduce_start(links, me, product, core_out, core_in):
    z, y, x, c = me
    core = []
    for i, d in enumerate(sum_order(z)):
        core_out[i] = product(4 + d).astype(jnp.bfloat16)
        core.append(links.go(core_out.at[i], core_in.at[i], device(z, y, x, 1 - c)))
    return core, []


def reduce_step(links, me, state, i, product, core_in, ring_out, ring_in):
    core, ring = state
    z, y, x, c = me
    following, _ = ring_of(z)
    mine = product(sum_order(z)[i])
    rows = mine.shape[0] // CHUNKS
    core[i].wait_recv()
    sent, last = [], []
    for h in range(CHUNKS):
        cut = slice(h * rows, (h + 1) * rows)
        here = pl.ds(h * rows, rows)
        value = mine[cut] + core_in[i, here, :].astype(jnp.float32)
        if i:
            ring[-1][h].wait_recv()
            value = value + ring_in[i - 1, here, :].astype(jnp.float32)
        if i < 3:
            ring_out[i, here, :] = value.astype(jnp.bfloat16)
            target = ring_in.at[i, here]
            sent.append(links.go(ring_out.at[i, here], target, device(following, y, x, c)))
        else:
            last.append(value)
    ring.append(sent)
    return last


def column_go(links, me, k, source, target):
    z, y, x, c = me
    own = z // 2 == c if k == 0 else None
    to = device(2 * c + flip(k, z % 2), y, x, z // 2)
    return links.go_unless(own, source, target, to)


def spread_go(links, me, k, source, full, send, recv):
    z, y, x, c = me
    rows = source.shape[0]
    first = pl.multiple_of((4 * c + 2 * flip(k, z % 2) + y) * rows, rows)
    target = full.at[pl.ds(first, rows), :]
    for dy in range(2):
        for dx in range(2):
            own = None if dy + dx else c == x
            to = device(z, flip(y, dy), flip(x, dx), x)
            links.go_unless(own, source, target, to, send.at[k, dy, dx], recv.at[k, dy, c])


def spread_wait(full, recv):
    rows = full.shape[0] // 8
    for k in range(2):
        for dy in range(2):
            for r in range(2):
                here = full.at[pl.ds(0, rows), :]
                pltpu.make_async_copy(here, here, recv.at[k, dy, r]).wait()


def join_go(links, me, k, grads, into, send, recv):
    z, y, x, c = me
    rows = into.shape[3]
    for dy in range(2):
        for r in range(2):
            block = 4 * r + 2 * flip(k, z % 2) + flip(y, dy)
            source = grads.at[pl.ds(pl.multiple_of(block * rows, rows), rows), :]
            own = None if dy else jnp.logical_and(c == x, c == r)
            to = device(z, flip(y, dy), c, r)
            links.go_unless(
                own, source, into.at[k, dy, x], to, send.at[k, dy, r], recv.at[k, dy, x]
            )


def join_sum(k, into, recv):
    total = 0.0
    for dy in range(2):
        for other in range(2):
            here = into.at[k, dy, other]
            pltpu.make_async_copy(here, here, recv.at[k, dy, other]).wait()
            total = total + into[k, dy, other].astype(jnp.float32)
    return total.astype(jnp.bfloat16)


def rms(rows):
    return lax.rsqrt(jnp.mean(rows * rows, axis=-1, keepdims=True) + epsilon)


def lane_sum(values):
    return jnp.sum(values, axis=-1, keepdims=True)


def head_of(z, y, x, c, heads):
    return 2 * c + z // 2, (z % 2) * (heads // 2) + 2 * x + y


def entry_kernel(
    lengths, tok_ref, cot_ref, small_ref, bucket_ref, wq_ref, wk_ref, wv_ref,
    rows_ref, normed, grads, pieces, weight, gain_one, gain_two, rev_ref,
    tok_in, cot_in, held, qkv, small, send, recv, plane_send, plane_recv,
):
    me = z, y, x, c = position()
    greet(*me)
    links = Links(send, recv)
    f, part, half = 2 * x + c, tok_in.shape[2], tok_in.shape[1]

    def gather_rows(ref, into):
        got = []
        for d in (1, 2, 3):
            xd, cd = flip(x, d // 2), flip(c, d % 2)
            source = ref.at[xd, pl.ds(pl.multiple_of(cd * half, half), half)]
            got.append(links.go(source, into.at[f], device(z, y, xd, cd)))
        into[f] = ref[x, pl.ds(pl.multiple_of(c * half, half), half), :]
        return got

    tok_got = gather_rows(tok_ref, tok_in)
    small[f, z, y] = small_ref[...]
    small_got = []
    for d in (1, 2, 3):
        here = small.at[f, z, y]
        small_got.append(links.go(here, here, device(flip_pair(z, d), y, x, c)))
    group_width = wq_ref.shape[1] // 2
    way = []
    for k in range(2):
        cut = pl.ds(pl.multiple_of(flip(k, z % 2) * group_width, group_width), group_width)
        for n, ref in enumerate((wq_ref, wk_ref, wv_ref)):
            target = held.at[k, :, n * group_width : (n + 1) * group_width]
            way.append(column_go(links, me, k, ref.at[:, cut], target))
    cot_got = gather_rows(cot_ref, cot_in)
    for made in small_got:
        made.wait_recv()
    here = small.at[f, :, y]
    links.go(here, here, device(z, 1 - y, x, c)).wait_recv()
    tables = []
    for d in (1, 2, 3):
        here = small.at[f]
        tables.append(links.go(here, here, device(z, y, flip(x, d // 2), flip(c, d % 2))))
    for i in range(4 * part // BLOCK):
        here = slice(i * BLOCK, (i + 1) * BLOCK)
        block = (i // 2) // 2, (i // 2) % 2
        gain_one[:, here] = small[f, block[0], block[1], i % 2 : i % 2 + 1, :]
        gain_two[:, here] = small[f, block[0], block[1], 2 + i % 2 : 3 + i % 2, :]
    for made in tok_got:
        made.wait_recv()
    wide = [tok_in[i].astype(jnp.float32) for i in range(4)]
    mean = sum(lane_sum(w * w) for w in wide) / (4 * part)
    scale = lax.rsqrt(mean + epsilon)
    for i in range(4):
        here = slice(i * part, (i + 1) * part)
        rows_ref[:, here] = tok_in[i]
        normed[0, :, here] = (wide[i] * scale * gain_one[:, here]).astype(jnp.bfloat16)
    first = share_start(links, normed, me)
    for made in cot_got:
        made.wait_recv()
    slot = (4 * z + 2 * y + c) * half + lax.broadcasted_iota(jnp.int32, (half, part), 0)
    valid = slot < jnp.where(x == 0, lengths[0], lengths[1])
    for i in range(4):
        grads[0, :, i * part : (i + 1) * part] = jnp.where(valid, cot_in[i], jnp.zeros_like(cot_in[i]))
    for k in range(2):
        for made in way[3 * k : 3 * k + 3]:
            made.wait_recv()
        spread_go(links, me, k, held.at[k], weight, plane_send, plane_recv)
    for step in (1, 2, 3):
        share_step(links, normed, me, first, step)
    second = share_start(links, grads, me)
    for made in tables:
        made.wait_recv()
    group = qkv.shape[1]
    heads = 2 * group
    source, place = head_of(z, y, x, c, heads)
    lane = lax.broadcasted_iota(jnp.int32, (1, BLOCK), 1)
    line = jnp.zeros(bucket_ref.shape, jnp.float32)
    per_block = 4
    for n in range(8 * per_block):
        block = n // per_block
        row = small[source, block // 2, block % 2, 4:5, :]
        value = lane_sum(jnp.where(lane == (n % per_block) * heads + place, row, 0.0))
        line = jnp.where(bucket_ref[...] == n, value, line)
    rev_ref[...] = line
    share_end(first)
    spread_wait(weight, plane_recv)
    count = 2 * normed.shape[1]

    @pl.loop(0, 4)
    def _(i):
        left = normed[pl.ds(2 * i, 2)].reshape(count, 4 * part)
        out = jnp.dot(left, weight[...], preferred_element_type=jnp.float32)
        out = out.astype(jnp.bfloat16).T
        qkv[:, :, :, lanes(i * count, count)] = out.reshape(3, group, DH, count)

    sent = []
    for d in (1, 2, 3):
        xd, yd = flip(x, d // 2), flip(y, d % 2)
        sent.append(links.go(qkv.at[:, 2 * xd + yd], pieces.at[d], device(z, yd, xd, c)))
    pieces[0] = qkv[:, 2 * x + y]
    for step in (1, 2, 3):
        share_step(links, grads, me, second, step)
    share_end(second)
    for made in sent:
        made.wait_recv()
    links.finish()


def low_array(*shape):
    return jax.ShapeDtypeStruct(shape, jnp.bfloat16)


def wide_array(*shape):
    return jax.ShapeDtypeStruct(shape, jnp.float32)


def low_space(*shape):
    return pltpu.VMEM(shape, jnp.bfloat16)


def entry(lengths, tokens_in, cotangent, small, rev_buckets, weights):
    _, slot_count, part = tokens_in.shape
    rows, width = slot_count // 2, 4 * part
    depth, cols = weights[0].shape
    group = cols // (2 * DH)
    wide = 3 * cols // 2
    return pl.pallas_call(
        entry_kernel,
        name="entry",
        out_shape=[
            low_array(rows, width),
            low_array(8, rows, width),
            low_array(8, rows, width),
            low_array(4, 3, DH, 8 * rows),
            low_array(8 * depth, wide),
            wide_array(1, width),
            wide_array(1, width),
            wide_array(*rev_buckets.shape),
        ],
        in_specs=[pl.BlockSpec(memory_space=pltpu.SMEM)] + [IN_VMEM] * 7,
        out_specs=[IN_VMEM] * 8,
        scratch_shapes=[
            low_space(4, rows, part),
            low_space(4, rows, part),
            low_space(2, depth, wide),
            low_space(3, group, DH, 8 * rows),
            pltpu.VMEM((4, 4, 2, 8, BLOCK), jnp.float32),
            COPIES((64,)),
            COPIES((64,)),
            COPIES((2, 2, 2)),
            COPIES((2, 2, 2)),
        ],
        compiler_params=pltpu.CompilerParams(
            collective_id=1, has_side_effects=True, vmem_limit_bytes=48 << 20
        ),
    )(lengths, tokens_in, cotangent, small, rev_buckets, *weights)


def middle_kernel(
    ctx_ref, rows_ref, gain_ref, slot0, slot1,
    normed, residual_ref, context, out_weight, gate_up, down,
    ctx_all, core_out, core_in, ring_out, ring_in, send, recv, plane_send, plane_recv,
):
    me = z, y, x, c = position()
    greet(*me)
    links = Links(send, recv)
    own = 2 * x + y
    heads = []
    for d in (1, 2, 3):
        xd, yd = flip(x, d // 2), flip(y, d % 2)
        heads.append(links.go(ctx_ref.at[d], ctx_all.at[own], device(z, yd, xd, c)))
    start = 0
    for n, full in enumerate((out_weight, gate_up, down)):
        cut = slice(start, start + full.shape[1])
        start = start + full.shape[1]
        for k, slot in enumerate((slot0, slot1)):
            spread_go(links, me, k, slot.at[:, cut], full, plane_send.at[n], plane_recv.at[n])
    ctx_all[own] = ctx_ref[0]
    for made in heads:
        made.wait_recv()
    group, size, tokens = ctx_all.shape
    context[...] = ctx_all[...].reshape(group * size, tokens).T
    spread_wait(out_weight, plane_recv.at[0])
    rows = tokens // 8

    def product(block):
        return right_transposed(
            context[pl.ds(pl.multiple_of(block * rows, rows), rows), :], out_weight[...]
        )

    state = reduce_start(links, me, product, core_out, core_in)
    for i in range(4):
        last = reduce_step(links, me, state, i, product, core_in, ring_out, ring_in)
    residual = rows_ref[...].astype(jnp.float32) + jnp.concatenate(last, axis=0)
    residual_ref[...] = residual
    gain = gain_ref[...].astype(jnp.float32)
    normed[0] = (residual * rms(residual) * gain).astype(jnp.bfloat16)
    shared = share_start(links, normed, me)
    for step in (1, 2, 3):
        share_step(links, normed, me, shared, step)
    share_end(shared)
    spread_wait(gate_up, plane_recv.at[1])
    spread_wait(down, plane_recv.at[2])
    links.finish()


def reduce_space(rows, width):
    return [
        low_space(4, rows, width),
        low_space(4, rows, width),
        low_space(3, rows, width),
        low_space(3, rows, width),
    ]


def middle(ctx_pieces, token_rows, gain, slots, widths):
    _, size, tokens = ctx_pieces.shape
    rows, width = token_rows.shape
    depth = slots[0].shape[0]
    return pl.pallas_call(
        middle_kernel,
        name="middle",
        out_shape=[
            low_array(8, rows, width),
            wide_array(rows, width),
            low_array(tokens, 4 * size),
            *(low_array(8 * depth, w) for w in widths),
        ],
        in_specs=[IN_VMEM] * 5,
        out_specs=[IN_VMEM] * 4 + [IN_PLACE] * 2,
        scratch_shapes=[
            low_space(4, size, tokens),
            *reduce_space(rows, width),
            COPIES((48,)),
            COPIES((48,)),
            COPIES((3, 2, 2, 2)),
            COPIES((3, 2, 2, 2)),
        ],
        compiler_params=pltpu.CompilerParams(
            collective_id=2, has_side_effects=True, vmem_limit_bytes=48 << 20
        ),
    )(ctx_pieces, token_rows, gain, *slots)


def back_kernel(
    pre_ref, weight_ref, residual_ref, own_ref, gain_ref, out_weight, grad_gu, grad_d,
    low_ref, wide_ref, part_ref, pieces, sum0, sum1,
    heads_out, in_gu, in_d, core_out, core_in, ring_out, ring_in, send, recv, plane_send, plane_recv,
):
    me = z, y, x, c = position()
    greet(*me)
    links = Links(send, recv)
    rows = residual_ref.shape[0]

    def product(block):
        return right_transposed(
            pre_ref[pl.ds(pl.multiple_of(block * rows, rows), rows), :], weight_ref[...]
        )

    for k in range(2):
        join_go(links, me, k, grad_gu, in_gu, plane_send.at[0], plane_recv.at[0])
        join_go(links, me, k, grad_d, in_d, plane_send.at[1], plane_recv.at[1])
    state = reduce_start(links, me, product, core_out, core_in)
    for i in range(4):
        last = reduce_step(links, me, state, i, product, core_in, ring_out, ring_in)
    normed_grad = jnp.concatenate(last, axis=0)
    residual = residual_ref[...]
    scale = rms(residual)
    unit = residual * scale
    part_ref[...] = jnp.sum(normed_grad * unit, axis=0, keepdims=True)
    out = own_ref[...].astype(jnp.float32) + norm_back(normed_grad, unit, scale, gain_ref[...])
    wide_ref[...] = out
    low_ref[0] = out.astype(jnp.bfloat16)
    shared = share_start(links, low_ref, me)
    for step in (1, 2, 3):
        share_step(links, low_ref, me, shared, step)
    share_end(shared)
    group, size, tokens = heads_out.shape
    count = 2 * rows
    for i in range(4):
        left = low_ref[2 * i : 2 * i + 2].reshape(count, low_ref.shape[2])
        out = jnp.dot(left, out_weight[...], preferred_element_type=jnp.float32)
        out = out.astype(jnp.bfloat16).T
        heads_out[:, :, i * count : (i + 1) * count] = out.reshape(group, size, count)
    heads = []
    for d in (1, 2, 3):
        xd, yd = flip(x, d // 2), flip(y, d % 2)
        heads.append(links.go(heads_out.at[2 * xd + yd], pieces.at[d], device(z, yd, xd, c)))
    pieces[0] = heads_out[2 * x + y]
    for made in heads:
        made.wait_recv()
    for k in range(2):
        wide = in_gu.shape[-1]
        (sum0, sum1)[k][:, :wide] = join_sum(k, in_gu, plane_recv.at[0])
        (sum0, sum1)[k][:, wide:] = join_sum(k, in_d, plane_recv.at[1])
    links.finish()


def back(grad_pre, gate_up, residual, grad_own, gain, out_weight, grad_gate_up, grad_down):
    rows, width = residual.shape
    group = out_weight.shape[1] // DH
    depth = gate_up.shape[0] // 8
    return pl.pallas_call(
        back_kernel,
        name="back",
        out_shape=[
            low_array(8, rows, width),
            wide_array(rows, width),
            wide_array(1, width),
            low_array(group, DH, 8 * rows),
            low_array(depth, grad_gate_up.shape[1] + grad_down.shape[1]),
            low_array(depth, grad_gate_up.shape[1] + grad_down.shape[1]),
        ],
        in_specs=[IN_VMEM] * 6 + [IN_PLACE] * 2,
        out_specs=[IN_VMEM] * 6,
        scratch_shapes=[
            low_space(group, DH, 8 * rows),
            low_space(2, 2, 2, depth, grad_gate_up.shape[1]),
            low_space(2, 2, 2, depth, grad_down.shape[1]),
            *reduce_space(rows, width),
            COPIES((48,)),
            COPIES((48,)),
            COPIES((2, 2, 2, 2)),
            COPIES((2, 2, 2, 2)),
        ],
        compiler_params=pltpu.CompilerParams(
            collective_id=3, has_side_effects=True, vmem_limit_bytes=56 << 20
        ),
    )(grad_pre, gate_up, residual, grad_own, gain, out_weight, grad_gate_up, grad_down)


def exit_kernel(
    piece_ref, normed_ref, weight_ref, token_ref, wide_ref, gain_ref, low_ref, context_ref,
    hidden_ref, down_ref, residual_ref, gain_two_ref, line_ref, bucket_ref,
    query_out, key_out, value_out, output_out, home_ref, layer_ref, small_ref,
    heads_in, rows_low, grad_qkv, grad_out, in_qkv, in_out, held, token_out, layer_own,
    packed, in_f, in_y, in_z,
    core_out, core_in, ring_out, ring_in, core_out2, core_in2, ring_out2, ring_in2,
    send, recv, plane_send, plane_recv,
):
    me = z, y, x, c = position()
    greet(*me)
    links = Links(send, recv)
    own, f = 2 * x + y, 2 * x + c
    group, three, size, tokens = heads_in.shape
    rows = tokens // 8
    depth = grad_qkv.shape[0] // 8
    width = normed_ref.shape[2]
    part = width // 4
    heads = []
    for d in (1, 2, 3):
        xd, yd = flip(x, d // 2), flip(y, d % 2)
        heads.append(links.go(piece_ref.at[d], heads_in.at[own], device(z, yd, xd, c)))
    heads_in[own] = piece_ref[0]

    def block_rows(ref, block):
        return ref[pl.ds(pl.multiple_of(block * rows, rows), rows), :]

    def ffn_product(block):
        return right_transposed(block_rows(hidden_ref, block), down_ref[...])

    def product(block):
        return right_transposed(block_rows(rows_low, block), weight_ref[...])

    def to_home(source, into):
        got = []
        for d in (1, 2, 3):
            xd, cd = flip(x, d // 2), flip(c, d % 2)
            got.append(links.go(source.at[2 * xd + cd], into.at[f], device(z, y, xd, cd)))
        into[f] = source[f]
        return got

    def ffn_step(i):
        return reduce_step(links, me, ffn, i, ffn_product, core_in2, ring_out2, ring_in2)

    def step(i):
        return reduce_step(links, me, state, i, product, core_in, ring_out, ring_in)

    ffn = reduce_start(links, me, ffn_product, core_out2, core_in2)
    ffn_step(0)
    for k in range(2):
        for n in range(4):
            block = 4 * (n // 2) + 2 * flip(k, z % 2) + n % 2
            here = pl.ds(pl.multiple_of(block * depth, depth), depth)
            left = low_ref[:, :, here].reshape(tokens, depth)
            grad_out[here, :] = left_transposed(left, context_ref[...]).astype(jnp.bfloat16)
        join_go(links, me, k, grad_out, in_out, plane_send.at[1], plane_recv.at[1])
    for made in heads:
        made.wait_recv()
    for n in range(three):
        here = slice(n * group * size, (n + 1) * group * size)
        rows_low[:, here] = heads_in[:, n].reshape(group * size, tokens).T
    state = reduce_start(links, me, product, core_out, core_in)
    step(0)
    ffn_step(1)
    for k in range(2):
        for n in range(4):
            block = 4 * (n // 2) + 2 * flip(k, z % 2) + n % 2
            here = pl.ds(pl.multiple_of(block * depth, depth), depth)
            left = normed_ref[:, :, here].reshape(tokens, depth)
            grad_qkv[here, :] = left_transposed(left, rows_low[...]).astype(jnp.bfloat16)
        join_go(links, me, k, grad_qkv, in_qkv, plane_send.at[0], plane_recv.at[0])
        step(1 + k)
        last = ffn_step(2 + k)
    layer = (residual_ref[...] + jnp.concatenate(last, axis=0)).astype(jnp.bfloat16)
    for i in range(4):
        layer_own[i] = layer[:, i * part : (i + 1) * part]
    home = to_home(layer_own, layer_ref)

    packed[...] = jnp.zeros_like(packed)
    per_block = 4
    all_heads = BLOCK // per_block
    source, place = head_of(z, y, x, c, all_heads // 4)
    lane = lax.broadcasted_iota(jnp.int32, (1, BLOCK), 1)
    for block in range(8):
        row = jnp.zeros((1, BLOCK), jnp.float32)
        for n in range(per_block):
            hot = bucket_ref[...] == block * per_block + n
            value = lane_sum(jnp.where(hot, line_ref[...], 0.0))
            row = jnp.where(lane == n * all_heads + source * (all_heads // 4) + place, value, row)
        packed[block // 2, block % 2, 4:5, :] = row
    last = step(3)
    normed_grad = jnp.concatenate(last, axis=0)
    tokens_wide = token_ref[...].astype(jnp.float32)
    scale = rms(tokens_wide)
    unit = tokens_wide * scale
    token_grad = wide_ref[...] + norm_back(normed_grad, unit, scale, gain_ref[...])
    for i in range(4):
        token_out[i] = token_grad[:, i * part : (i + 1) * part].astype(jnp.bfloat16)
    home += to_home(token_out, home_ref)
    gain_part = jnp.sum(normed_grad * unit, axis=0, keepdims=True)
    for i in range(width // BLOCK):
        here = slice(i * BLOCK, (i + 1) * BLOCK)
        block = (i // 2) // 2, (i // 2) % 2
        packed[block[0], block[1], i % 2 : i % 2 + 1, :] = gain_part[:, here]
        packed[block[0], block[1], 2 + i % 2 : 3 + i % 2, :] = gain_two_ref[:, here]
    got = []
    for d in (1, 2, 3):
        to = device(z, y, flip(x, d // 2), flip(c, d % 2))
        got.append(links.go(packed, in_f.at[d - 1], to))
    wide_qkv = in_qkv.shape[-1]
    group_width = wide_qkv // 3
    cut = pl.ds(pl.multiple_of((z % 2) * group_width, group_width), group_width)
    way = []
    for k in range(2):
        held[k, :, :wide_qkv] = join_sum(k, in_qkv, plane_recv.at[0])
        held[k, :, wide_qkv:] = join_sum(k, in_out, plane_recv.at[1])
        for n, ref in enumerate((query_out, key_out, value_out, output_out)):
            sent = held.at[k, :, n * group_width : (n + 1) * group_width]
            way.append(column_go(links, me, k, sent, ref.at[:, cut]))
    for made in got:
        made.wait_recv()
    for made in got:
        links.done(made)
    packed[...] = packed[...] + in_f[0] + in_f[1] + in_f[2]
    made = links.go(packed.at[:, 1 - y], in_y, device(z, 1 - y, x, c))
    made.wait_recv()
    in_y[...] = in_y[...] + packed[:, y]
    got = []
    for d in (1, 2, 3):
        other = flip_pair(z, d)
        got.append(links.go(in_y.at[other], in_z.at[d - 1], device(other, y, x, c)))
    for made in got:
        made.wait_recv()
    small_ref[...] = in_y[z] + in_z[0] + in_z[1] + in_z[2]
    for made in way + home:
        made.wait_recv()
    links.finish()


def leave(pieces, normed, weight, token_rows, wide_grad, gain, low, context, hidden, down, residual,
          gain_two_part, line_grad, rev_buckets):
    _, _, size, tokens = pieces.shape
    rows, width = token_rows.shape
    depth, wide = weight.shape[0] // 8, weight.shape[1]
    out_wide = context.shape[1]
    cols = 2 * wide // 3
    tile = (8, BLOCK)
    return pl.pallas_call(
        exit_kernel,
        name="leave",
        out_shape=[
            *(low_array(depth, cols) for _ in range(4)),
            low_array(4, rows, width // 4),
            low_array(4, rows, width // 4),
            wide_array(*tile),
        ],
        in_specs=[IN_VMEM] * 14,
        out_specs=[IN_VMEM] * 7,
        scratch_shapes=[
            low_space(4, 3, size, tokens),
            low_space(tokens, wide),
            low_space(8 * depth, wide),
            low_space(8 * depth, out_wide),
            low_space(2, 2, 2, depth, wide),
            low_space(2, 2, 2, depth, out_wide),
            low_space(2, depth, wide + out_wide),
            low_space(4, rows, width // 4),
            low_space(4, rows, width // 4),
            pltpu.VMEM((4, 2, *tile), jnp.float32),
            pltpu.VMEM((3, 4, 2, *tile), jnp.float32),
            pltpu.VMEM((4, *tile), jnp.float32),
            pltpu.VMEM((3, *tile), jnp.float32),
            *reduce_space(rows, width),
            *reduce_space(rows, width),
            COPIES((64,)),
            COPIES((64,)),
            COPIES((2, 2, 2, 2)),
            COPIES((2, 2, 2, 2)),
        ],
        compiler_params=pltpu.CompilerParams(
            collective_id=4, has_side_effects=True, vmem_limit_bytes=60 << 20
        ),
    )(pieces, normed, weight, token_rows, wide_grad, gain, low, context, hidden, down, residual,
      gain_two_part, line_grad, rev_buckets)


def fast_shards(
    tokens_in,
    cotangent,
    gain_attn,
    query_weight,
    key_weight,
    value_weight,
    output_weight,
    bias_table,
    gain_ffn,
    gate_weight,
    up_weight,
    down_weight,
    lengths,
    buckets,
):
    seq_index, fsdp_index = lax.axis_index("seq"), lax.axis_index("fsdp")
    z, y, x, c = seq_index // 2, seq_index % 2, fsdp_index // 2, fsdp_index % 2
    z_low, z_high = z % 2, z // 2
    batch_count, slot_count, part_width = tokens_in.shape
    width = part_width * 4
    row_count = query_weight.shape[0]
    heads = query_weight.shape[1] // DH
    group_heads = heads // 2
    group_width = group_heads * DH
    hidden_width = gate_weight.shape[1] // 2
    def halves(weights):
        slots = []
        for k in range(2):
            half = k ^ z_low
            slots.append(
                jnp.concatenate(
                    [
                        lax.dynamic_slice_in_dim(w, half * (w.shape[1] // 2), w.shape[1] // 2, 1)
                        for w in weights
                    ],
                    axis=1,
                )
            )
        return slots

    small = jnp.concatenate(
        [gain_attn, gain_ffn, bias_table.reshape(-1), jnp.zeros((2 * row_count - bias_table.size,), jnp.bfloat16)]
    )
    small = small.astype(jnp.float32).reshape(8, BLOCK)
    rev_buckets = jnp.concatenate([buckets[::-1], jnp.full((1,), -1, jnp.int32)])[None, :]
    token_low, normed_one, grad_rows, pieces, qkv_weight, gain_one, gain_two, rev_line = entry(
        lengths,
        tokens_in,
        cotangent,
        small,
        rev_buckets,
        (query_weight, key_weight, value_weight),
    )
    tokens = 4 * slot_count
    grad_own = grad_rows[0]
    later = halves([output_weight, gate_weight, up_weight, down_weight])
    pieces, *later = lax.optimization_barrier((pieces, *later))
    held = [move(later[k], spread_slot(k)) for k in range(2)]
    context_pieces, context_wide, lse, qkv_all = attend(lengths, pieces, rev_line)
    normed_two, residual, context, output_full, gate_up, down_full = middle(
        context_pieces, token_low, gain_two, held, (group_width, 2 * hidden_width, hidden_width)
    )
    normed_two = normed_two.reshape(tokens, width)
    grad_rows = grad_rows.reshape(tokens, width)
    gate_up_pre = plain_product(normed_two, gate_up)
    gate_pre, up_pre = gate_up_pre[:, :hidden_width], gate_up_pre[:, hidden_width:]
    activated, gelu_back = jax.vjp(jax.nn.gelu, gate_pre)
    hidden = (activated * up_pre).astype(jnp.bfloat16)
    grad_hidden = plain_product(grad_rows, down_full)
    grad_pre = jnp.concatenate(
        [
            gelu_back(grad_hidden * up_pre)[0].astype(jnp.bfloat16),
            (grad_hidden * activated).astype(jnp.bfloat16),
        ],
        axis=1,
    )
    grad_gate_up = left_transposed(normed_two, grad_pre).astype(jnp.bfloat16)
    grad_down = left_transposed(grad_rows, hidden).astype(jnp.bfloat16)
    residual_low, residual_grad, gain_two_part, grad_pieces, *sums = back(
        grad_pre, gate_up, residual, grad_own, gain_two, output_full, grad_gate_up, grad_down
    )
    ffn_slots = [move(sums[k], spread_slot(k)) for k in range(2)]
    qkv_grad_pieces, line_grad = attend_back(
        lengths, grad_pieces, rev_line, context_wide, lse, qkv_all
    )
    qkv_grad_pieces, *ffn_slots = lax.optimization_barrier((qkv_grad_pieces, *ffn_slots))
    *attn_sums, home, layer, small = leave(
        qkv_grad_pieces,
        normed_one,
        qkv_weight,
        token_low,
        residual_grad,
        gain_one,
        residual_low,
        context,
        hidden,
        down_full,
        residual,
        gain_two_part,
        line_grad,
        rev_buckets,
    )
    token_share = home.astype(jnp.float32).reshape(batch_count, slot_count, part_width)
    layer_out = layer.reshape(batch_count, slot_count, part_width)

    def own_columns(first, size):
        cut = [s[:, first : first + size].astype(jnp.float32) for s in ffn_slots]
        return jnp.concatenate(
            [jnp.where(z_low == 0, cut[0], cut[1]), jnp.where(z_low == 0, cut[1], cut[0])], axis=1
        )

    query_sum, key_sum, value_sum, output_sum = (s.astype(jnp.float32) for s in attn_sums)
    gate_sum, up_sum, down_sum = (own_columns(i * hidden_width, hidden_width) for i in range(3))
    table_sum = lax.dynamic_slice_in_dim(
        small[4].reshape(-1, 4 * heads), fsdp_index * heads, heads, 1
    )
    return (
        layer_out,
        token_share,
        small[:2].reshape(-1),
        query_sum,
        key_sum,
        value_sum,
        output_sum,
        table_sum,
        small[2:4].reshape(-1),
        gate_sum,
        up_sum,
        down_sum,
    )


def solution(mesh):
    placed = (
        P(None, "seq", "fsdp"),
        P(None, "seq", "fsdp"),
        P("seq"),
        P("seq", "fsdp"),
        P("seq", "fsdp"),
        P("seq", "fsdp"),
        P("seq", "fsdp"),
        P("seq", "fsdp"),
        P("seq"),
        P("seq", "fsdp"),
        P("seq", "fsdp"),
        P("seq", "fsdp"),
        P(),
        P(),
    )
    return jax.shard_map(
        fast_shards if (mesh.shape["seq"], mesh.shape["fsdp"]) == (8, 4) else shards,
        mesh=mesh,
        in_specs=placed,
        out_specs=(
            P(None, "seq", "fsdp"),
            P(None, "seq", "fsdp"),
            P("seq"),
            P("seq", "fsdp"),
            P("seq", "fsdp"),
            P("seq", "fsdp"),
            P("seq", "fsdp"),
            P("seq", "fsdp"),
            P("seq"),
            P("seq", "fsdp"),
            P("seq", "fsdp"),
            P("seq", "fsdp"),
        ),
        check_vma=False,
    )
```

profile of v0, /device:TPU:0, one launch (start us, length us, event | category | flops | bytes accessed | tf_op | source)
XLA Modules:
  0.0 603.7 jit_solution(9019589241409374201)
XLA Ops:
  0.7 0.8 reshape.52
  1.5 0.8 reverse
  2.3 0.1 slice.79
  2.4 0.1 pad_add_fusion
  2.5 1.1 constant_dynamic-slice_fusion.3
  3.6 1.4 constant_dynamic-slice_fusion.1
  5.0 0.0 copy-start.5
  5.0 0.0 copy-start.7
  5.0 0.0 copy-start.8
  5.2 0.1 fusion.7.small_ref
  5.2 1.1 pad_maximum_fusion.5
  6.3 1.1 pad_maximum_fusion.4
  7.4 99.8 %entry.1 = (bf16[128,2048]{1,0:T(8,128)(2,1)S(1)}, bf16[8,128,2048]{2,1,0:T(8,128)(2,1)}, bf16[8,128,2048]{2,1,0:T(8,128)(2,1)}, bf16[4,3,64,1024]{3,2,1,0:T(8,1...) custom-call(s32[2]{0:T(128)S(1)} %copy-done.14, ...), custom_call_target="tpu_custom_call" | custom-call | tf_op jit(solution)/shard_map/entry/pallas_call | solution.py:982
  107.3 0.6 copy-done.13
  107.9 1.9 collective-permute-start
  109.8 0.1 collective-permute-start.1
  109.9 49.8 %attend.1 = (bf16[4,64,1024]{2,1,0:T(8,128)(2,1)S(1)}, f32[2,64,2048]{2,1,0:T(8,128)S(1)}, f32[2,1,2048]{2,1,0:T(1,128)S(1)}, bf16[2,3,64,2048]{3,2,1,0:T(8,128)(2,1)S(1)}) custom-call(s32[2]{0:T(128)S(1)} %copy-done.14, bf16[4,3,64,1024]{3,2,1,0:T(8,128)(2,1)S(1)} %get-tuple-element.53.pieces, f32[1,4096]{1,0:T(1,128)S(1)} %get-tuple-element.54.rev_ref), custom_call_target="tpu_custom_call" | custom-call | flops 46000001024 | bytes 4194304 | tf_op jit(solution)/shard_map/attend/pallas_call | solution.py:479
  159.7 1.1 copy-done.16
  160.8 1.0 copy-done.18
  161.8 1.9 slice_bitcast_fusion.own_ref
  163.7 109.4 %middle.1 = (bf16[8,128,2048]{2,1,0:T(8,128)(2,1)}, f32[128,2048]{1,0:T(8,128)S(1)}, bf16[1024,256]{1,0:T(8,128)(2,1)S(1)}, bf16[2048,256]{1,0:T(8,128)(2,1)S(1)...) custom-call(bf16[4,64,1024]{2,1,0:T(8,128)(2,1)S(1)} %get-tuple-element.55.ctx_ref, ...), custom_call_target="tpu_custom_call" | custom-call | tf_op jit(solution)/shard_map/middle/pallas_call | solution.py:1075
  273.2 10.6 %fusion.8 = f32[1024,1280]{1,0:T(8,128)S(1)} fusion(bf16[1024,2048]{1,0:T(8,128)(2,1)} %bitcast.34, bf16[2048,1280]{1,0:T(8,128)(2,1)} %get-tuple-element.62.weight_ref), kind=kOutput, calls=%fused_computation.43 | convolution fusion | flops 5368709120 | bytes 14680064 | tf_op jit(solution)/shard_map/dot_general | solution.py:19
  283.8 4.9 fusion.6
  288.8 7.7 %convolution_convert_fusion.grad_gu = bf16[2048,1280]{1,0:T(8,128)(2,1)} fusion(bf16[1024,2048]{1,0:T(8,128)(2,1)S(1)} %bitcast.35, bf16[1024,640]{1,0:T(8,128)(2,1)S(1)} %get-tuple-element.91, bf16[1024,640]{1,0:T(8,128)(2,1)S(1)} %get-tuple-element.90), kind=kOutput, calls=%fused_computation | convolution fusion | flops 5376573440 | bytes 12058624 | tf_op jit(solution)/shard_map/dot_general | solution.py:29
  296.5 1.8 pad_maximum_fusion.pre_ref
  298.2 5.0 convolution_convert_fusion.1.grad_d
  303.3 108.3 %back.1 = (bf16[8,128,2048]{2,1,0:T(8,128)(2,1)}, f32[128,2048]{1,0:T(8,128)}, f32[1,2048]{1,0:T(1,128)}, bf16[4,64,1024]{2,1,0:T(8,128)(2,1)}, bf16[256,1920]{1,0:T(8,128)(2,1)}, /*index=5*/bf16[256,1920]{1,0:T(8,128)(2,1)}) custom-call(bf16[1024,1280]{1,0:T(8,128)(2,1)} %pad_maximum_fusion.pre_ref, bf16[2048,1280]{1,0:T(8,128)(2,1)} %get-tuple-element.62.weight_ref, ...), custom_call_target="tpu_custom_call" | custom-call | tf_op jit(solution)/shard_map/back/pallas_call | solution.py:1158
  411.6 2.0 collective-permute-start.2
  413.6 0.7 collective-permute-start.3
  414.3 1.0 copy-done.15
  415.4 48.2 %attend_back.1 = (bf16[4,3,64,1024]{3,2,1,0:T(8,128)(2,1)S(1)}, f32[1,4096]{1,0:T(1,128)S(1)}) custom-call(s32[2]{0:T(128)S(1)} %copy-done.14, bf16[4,64,1024]{2,1,0:T(8,128)(2,1)S(1)} %copy-done.15, f32[1,4096]{1,0:T(1,128)S(1)} %get-tuple-element.54.rev_ref, f32[2,64,2048]{2,1,0:T(8,128)S(1)} %copy-done.19, f32[2,1,2048]{2,1,0:T(1,128)S(1)} %get-tuple-element.67.lse_ref, ...), custom_call_target="tpu_custom_call" | custom-call | flops 46000001024 | bytes 4194304 | tf_op jit(solution)/shard_map/attend_back/pallas_call | solution.py:600
  463.6 1.2 copy-done.2
  464.8 0.6 copy-done.12
  465.4 123.0 %leave.1 = (bf16[256,512]{1,0:T(8,128)(2,1)}, bf16[256,512]{1,0:T(8,128)(2,1)}, bf16[256,512]{1,0:T(8,128)(2,1)}, bf16[256,512]{1,0:T(8,128)(2,1)}, bf16[4,128,5...) custom-call(bf16[4,3,64,1024]{3,2,1,0:T(8,128)(2,1)} %copy-done.2, ...), custom_call_target="tpu_custom_call" | custom-call | tf_op jit(solution)/shard_map/leave/pallas_call | solution.py:1334
  588.4 0.8 slice_reduce_fusion
  589.2 1.3 slice_bitcast_fusion.1
  590.5 0.1 reshape_squeeze.3
  590.6 2.1 bitcast_convert_fusion
  592.7 1.8 convert_element_type.60
  594.5 1.8 convert_element_type.61
  596.3 0.9 convert_element_type.62
  597.2 0.9 convert_element_type.63
  598.0 0.6 constant_dynamic-slice_fusion
  598.7 0.3 convert_select_fusion.1
  599.0 1.1 pad_maximum_fusion.3
  600.1 1.1 pad_maximum_fusion.1
  601.2 1.1 pad_maximum_fusion.2
  602.4 0.8 copy.30
  (57 shorter events, 0.2 us)
Async XLA Ops:
  0.6 4.4 copy-start.25
  0.7 4.5 copy-start.27
  0.7 4.5 copy-start.28
  2.5 4.9 copy-start.10
  5.0 2.4 copy-start.5
  5.0 2.4 copy-start.6
  5.0 2.4 copy-start.7
  5.0 2.3 copy-start.8
  5.1 2.3 copy-start.9
  5.1 2.3 copy-start.14
  107.3 0.6 copy-start.13
  107.9 55.8 %copy-start.1 = (bf16[128,2048]{1,0:T(8,128)(2,1)}, bf16[128,2048]{1,0:T(8,128)(2,1)S(1)}, u32[]{:S(2)}) copy-start(bf16[128,2048]{1,0:T(8,128)(2,1)S(1)} %get-tuple-element.56.rows_ref.token_ref) | copy-start | bytes 1572868
  107.9 55.8 %copy-start.11 = (f32[1,2048]{1,0:T(1,128)}, f32[1,2048]{1,0:T(1,128)S(1)}, u32[]{:S(2)}) copy-start(f32[1,2048]{1,0:T(1,128)S(1)} %get-tuple-element.57.gain_ref) | copy-start | bytes 24580
  107.9 55.8 %collective-permute-start = (bf16[256,2176]{1,0:T(8,128)(2,1)}, bf16[256,2176]{1,0:T(8,128)(2,1)S(1)}, u32[]{:S(2)}, u32[]{:S(2)}) collective-permute-start(bf16[256,2176]{1,0:T(8,128)(2,1)} %pad_maximum_fusion.4), channel_id=1, source_target_pairs={{0,0},{1,16},{2,2},{3,18},{4,4},{5,20},{6,6},{7,22},{8,8},{9,24},{... | collective-permute-start | bytes 3342344 | tf_op jit(solution)/shard_map/ppermute | solution.py:326
  109.8 53.9 %collective-permute-start.1 = (bf16[256,2176]{1,0:T(8,128)(2,1)}, bf16[256,2176]{1,0:T(8,128)(2,1)S(1)}, u32[]{:S(2)}, u32[]{:S(2)}) collective-permute-start(bf16[256,2176]{1,0:T(8,128)(2,1)} %pad_maximum_fusion.5), channel_id=1, source_target_pairs={{0,8},{1,24},{2,10},{3,26},{4,12},{5,28},{6,14},{7,30},{8,0},{9,16... | collective-permute-start | bytes 3342344 | tf_op jit(solution)/shard_map/ppermute | solution.py:326
  159.7 1.1 copy-start.16
  160.8 1.0 copy-start.18
  273.1 10.7 %copy-start = (f32[128,2048]{1,0:T(8,128)}, f32[128,2048]{1,0:T(8,128)S(1)}, u32[]{:S(2)}) copy-start(f32[128,2048]{1,0:T(8,128)S(1)} %get-tuple-element.63.residual_ref) | copy-start | bytes 3145732
  273.1 10.7 %copy-start.3 = (bf16[2048,256]{1,0:T(8,128)(2,1)}, bf16[2048,256]{1,0:T(8,128)(2,1)S(1)}, u32[]{:S(2)}) copy-start(bf16[2048,256]{1,0:T(8,128)(2,1)S(1)} %get-tuple-element.64.out_weight) | copy-start | bytes 3145732
  273.1 10.7 %copy-start.4 = (bf16[1024,256]{1,0:T(8,128)(2,1)}, bf16[1024,256]{1,0:T(8,128)(2,1)S(1)}, u32[]{:S(2)}) copy-start(bf16[1024,256]{1,0:T(8,128)(2,1)S(1)} %get-tuple-element.78.context_ref) | copy-start | bytes 1572868
  273.1 10.7 %copy-start.20 = (bf16[2048,640]{1,0:T(8,128)(2,1)S(1)}, bf16[2048,640]{1,0:T(8,128)(2,1)}, u32[]{:S(2)}) copy-start(bf16[2048,640]{1,0:T(8,128)(2,1)} %get-tuple-element.60.down_ref) | copy-start | bytes 7864324
  273.2 10.7 %copy-start.26 = (bf16[8,128,2048]{2,1,0:T(8,128)(2,1)S(1)}, bf16[8,128,2048]{2,1,0:T(8,128)(2,1)}, u32[]{:S(2)}) copy-start(bf16[8,128,2048]{2,1,0:T(8,128)(2,1)} %get-tuple-element.51) | copy-start | bytes 12582916
  283.8 5.0 copy-start.29
  288.8 9.4 %copy-start.21 = (bf16[1024,640]{1,0:T(8,128)(2,1)}, bf16[1024,640]{1,0:T(8,128)(2,1)S(1)}, u32[]{:S(2)}) copy-start(bf16[1024,640]{1,0:T(8,128)(2,1)S(1)} %get-tuple-element.92.hidden_ref) | copy-start | bytes 3932164
  303.3 111.0 %copy-start.17 = (bf16[2,3,64,2048]{3,2,1,0:T(8,128)(2,1)S(1)}, bf16[2,3,64,2048]{3,2,1,0:T(8,128)(2,1)}, u32[]{:S(2)}) copy-start(bf16[2,3,64,2048]{3,2,1,0:T(8,128)(2,1)} %copy-done.16) | copy-start | bytes 4718596
  303.3 111.0 %copy-start.19 = (f32[2,64,2048]{2,1,0:T(8,128)S(1)}, f32[2,64,2048]{2,1,0:T(8,128)}, u32[]{:S(2)}) copy-start(f32[2,64,2048]{2,1,0:T(8,128)} %copy-done.18) | copy-start | bytes 3145732
  411.6 53.8 %collective-permute-start.2 = (bf16[256,1920]{1,0:T(8,128)(2,1)}, bf16[256,1920]{1,0:T(8,128)(2,1)S(1)}, u32[]{:S(2)}, u32[]{:S(2)}) collective-permute-start(bf16[256,1920]{1,0:T(8,128)(2,1)} %get-tuple-element.70), channel_id=1, source_target_pairs={{0,0},{1,16},{2,2},{3,18},{4,4},{5,20},{6,6},{7,22},{8,8},{9,24},{... | collective-permute-start | bytes 2949128 | tf_op jit(solution)/shard_map/ppermute | solution.py:326
  413.6 51.7 %collective-permute-start.3 = (bf16[256,1920]{1,0:T(8,128)(2,1)}, bf16[256,1920]{1,0:T(8,128)(2,1)S(1)}, u32[]{:S(2)}, u32[]{:S(2)}) collective-permute-start(bf16[256,1920]{1,0:T(8,128)(2,1)} %get-tuple-element.71), channel_id=1, source_target_pairs={{0,8},{1,24},{2,10},{3,26},{4,12},{5,28},{6,14},{7,30},{8,0},{9,16... | collective-permute-start | bytes 2949128 | tf_op jit(solution)/shard_map/ppermute | solution.py:326
  414.3 1.0 copy-start.15
  463.6 1.2 copy-start.2
  464.8 0.6 copy-start.12
  588.4 7.9 %copy-start.24 = (bf16[256,512]{1,0:T(8,128)(2,1)S(1)}, bf16[256,512]{1,0:T(8,128)(2,1)}, u32[]{:S(2)}) copy-start(bf16[256,512]{1,0:T(8,128)(2,1)} %get-tuple-element.86) | copy-start | bytes 786436
  588.4 8.8 %copy-start.23 = (bf16[256,512]{1,0:T(8,128)(2,1)S(1)}, bf16[256,512]{1,0:T(8,128)(2,1)}, u32[]{:S(2)}) copy-start(bf16[256,512]{1,0:T(8,128)(2,1)} %get-tuple-element.87) | copy-start | bytes 786436
  600.1 2.3 copy-start.22
where the time goes:
time: 603 us; the launch traced here: 604 us
  Pallas kernels  539 us (89%)
  matrix products  28.3 us (5%)
  local copies, waits for them, and re-layouts  15.3 us (3%)
  other arithmetic  15.2 us (3%)
    pallas_call x1, Pallas kernels, leave(): pl.pallas_call(exit_kernel, name='leave', out_shape=[*(low_array(depth, c...  123 us
    pallas_call x1, Pallas kernels, middle(): pl.pallas_call(middle_kernel, name='middle', out_shape=[low_array(8, rows...  109 us
    pallas_call x1, Pallas kernels, back(): pl.pallas_call(back_kernel, name='back', out_shape=[low_array(8, rows, wi...  108 us
    pallas_call x1, Pallas kernels, entry(): pl.pallas_call(entry_kernel, name='entry', out_shape=[low_array(rows, wid...  99.8 us
    pallas_call x1, Pallas kernels, attend(): pl.pallas_call(attend_kernel, name='attend', out_shape=[jax.ShapeDtypeStr...  49.8 us
    pallas_call x1, Pallas kernels, attend_back(): pl.pallas_call(attend_back_kernel, name='attend_back', out_shape=[jax.Sha...  48.2 us
    dot_general x2, matrix products, plain_product(): return jnp.dot(left, right, preferred_element_type=jnp.float32)  15.6 us
    dot_general x2, matrix products, left_transposed(): lax.dot_general(left, right, (((0,), (0,)), ((), ())), preferred_element_...  12.7 us
  transfers between devices with their start and end apart: 4, of which 0 were waited for; matrix products, arithmetic and copies ran while one was open for 0% of the time, Pallas kernels for 16%

commit v1 on v0

--- a/solution.py
+++ b/solution.py
@@ -13,6 +13,7 @@
 epsilon = 1e-06
 highest = lax.Precision.HIGHEST
 masked_score = -1e30
+root_two_over_pi = 0.7978845608028654
 
 
 def plain_product(left, right):
@@ -330,51 +331,9 @@
     return lambda z, y, x, c: (2 * c + (k ^ (z & 1)), y, x, z >> 1)
 
 
-def spread_plane(dy, dx):
-    return lambda z, y, x, c: (z, y ^ dy, c ^ dx, x)
-
-
-def join_plane(dy, dx):
-    return lambda z, y, x, c: (z, y ^ dy, c, x ^ dx)
-
-
-def along_z(d):
-    return lambda z, y, x, c: (z ^ d, y, x, c)
-
-
-def other_core(z, y, x, c):
-    return (z, y, x, c ^ 1)
-
-
-def across(dx, dy):
-    return lambda z, y, x, c: (z, y ^ dy, x ^ dx, c)
-
-
-def across_fsdp(d):
-    return lambda z, y, x, c: (z, y, x ^ (d >> 1), c ^ (d & 1))
-
-
-def in_place(relative, me):
-    current, bit = list(relative), 1
-    while bit < len(current):
-        swap = (me & bit) != 0
-        current = [jnp.where(swap, current[i ^ bit], current[i]) for i in range(len(current))]
-        bit *= 2
-    return current
-
-
-def sum_rows(mine, other):
-    mine = mine + move(other, other_core).astype(jnp.float32)
-    count = mine.shape[0] // 4
-    total = mine[:count]
-    for d in (1, 2, 3):
-        part = mine[d * count : (d + 1) * count].astype(jnp.bfloat16)
-        total = total + move(part, along_z(d)).astype(jnp.float32)
-    return total
-
-
-KEYS = 256
-QUERIES = 256
+KEYS = 512
+QUERIES = 512
+WIDE_QUERIES = 1024
 OFFSET = 1920
 
 
@@ -422,10 +381,10 @@
         valid = sc[b]
         full = valid // KEYS
 
-        @pl.loop(0, length // QUERIES)
+        @pl.loop(0, length // WIDE_QUERIES)
         def _(i):
-            first_query = i * QUERIES
-            query = qkv[b, 0, :, lanes(first_query, QUERIES)]
+            first_query = i * WIDE_QUERIES
+            query = qkv[b, 0, :, lanes(first_query, WIDE_QUERIES)]
 
             def tile(j, carry, masked):
                 peak, total, acc = carry
@@ -435,13 +394,13 @@
                 )
                 score = score + jnp.concatenate(
                     [
-                        table[:, lanes(first_query - first_key + OFFSET - t, QUERIES)]
+                        table[:, lanes(first_query - first_key + OFFSET - t, WIDE_QUERIES)]
                         for t in range(0, KEYS, BLOCK)
                     ],
                     axis=0,
                 )
                 if masked:
-                    position = first_key + lax.broadcasted_iota(jnp.int32, (KEYS, QUERIES), 0)
+                    position = first_key + lax.broadcasted_iota(jnp.int32, (KEYS, WIDE_QUERIES), 0)
                     score = jnp.where(position < valid, score, masked_score)
                 now = jnp.maximum(peak, jnp.max(score, axis=0, keepdims=True))
                 scale = jnp.exp(peak - now)
@@ -455,20 +414,20 @@
                 return now, total, acc
 
             carry = (
-                jnp.full((1, QUERIES), masked_score, jnp.float32),
-                jnp.zeros((1, QUERIES), jnp.float32),
-                jnp.zeros((DH, QUERIES), jnp.float32),
+                jnp.full((1, WIDE_QUERIES), masked_score, jnp.float32),
+                jnp.zeros((1, WIDE_QUERIES), jnp.float32),
+                jnp.zeros((DH, WIDE_QUERIES), jnp.float32),
             )
             carry = lax.fori_loop(0, full, lambda j, s: tile(j, s, False), carry)
             peak, total, acc = lax.cond(
                 valid > full * KEYS, lambda s: tile(full, s, True), lambda s: s, carry
             )
             context = acc / total
-            ctx_wide[b, :, lanes(first_query, QUERIES)] = context
-            lse_ref[b, :, lanes(first_query, QUERIES)] = peak + jnp.log(total)
+            ctx_wide[b, :, lanes(first_query, WIDE_QUERIES)] = context
+            lse_ref[b, :, lanes(first_query, WIDE_QUERIES)] = peak + jnp.log(total)
             low = context.astype(jnp.bfloat16)
-            for t in range(QUERIES // BLOCK):
-                piece, part = part_of(b, i * (QUERIES // BLOCK) + t, z, y, x, c)
+            for t in range(WIDE_QUERIES // BLOCK):
+                piece, part = part_of(b, i * (WIDE_QUERIES // BLOCK) + t, z, y, x, c)
                 ctx_ref[piece, :, lanes(part * BLOCK, BLOCK)] = low[:, t * BLOCK : (t + 1) * BLOCK]
 
 
@@ -527,7 +486,7 @@
     for b in range(2):
         valid = sc[b]
         full = valid // KEYS
-        count = (valid + KEYS - 1) // KEYS
+        count = (valid + QUERIES - 1) // QUERIES
 
         def key_step(j, masked):
             first_key = j * KEYS
@@ -703,6 +662,14 @@
         self.sent.append((own, made))
         return made
 
+    def go_if(self, there, here, source, target, send, recv, to):
+        made = remote(source, target, send, recv, to)
+        pl.when(there)(lambda: made.start())
+        if here is not None:
+            local = pltpu.make_async_copy(source, target, recv)
+            pl.when(here)(lambda: local.start())
+        self.sent.append((jnp.logical_not(there), made))
+
     def done(self, made):
         made.wait_send()
         self.sent = [m for m in self.sent if m is not made]
@@ -756,22 +723,322 @@
     return [flip_pair(z, b) for b in back] + [0]
 
 
-def reduce_start(links, me, product, core_out, core_in):
+def column_go(links, me, k, source, target):
     z, y, x, c = me
-    core = []
-    for i, d in enumerate(sum_order(z)):
-        core_out[i] = product(4 + d).astype(jnp.bfloat16)
-        core.append(links.go(core_out.at[i], core_in.at[i], device(z, y, x, 1 - c)))
-    return core, []
-
-
-def reduce_step(links, me, state, i, product, core_in, ring_out, ring_in):
-    core, ring = state
+    own = z // 2 == c if k == 0 else None
+    to = device(2 * c + flip(k, z % 2), y, x, z // 2)
+    return links.go_unless(own, source, target, to)
+
+
+def arrived(place, sem):
+    pltpu.make_async_copy(place, place, sem).wait()
+
+
+def spread_go(links, me, k, source, full, send, recv):
+    z, y, x, c = me
+    rows = source.shape[0]
+    first = pl.multiple_of((4 * c + 2 * flip(k, z % 2) + y) * rows, rows)
+    target = full.at[pl.ds(first, rows), :]
+    for dy, dx in ((0, 1), (1, 0), (0, 0)):
+        own = None if dy + dx else c == x
+        to = device(z, flip(y, dy), flip(x, dx), x)
+        links.go_unless(own, source, target, to, send.at[k, dy, dx], recv.at[k, dy, c])
+
+
+def spread_relay(links, me, full, send, recv):
+    z, y, x, c = me
+    odd = flip(c, x)
+    k, step = 1 - odd, 1 - odd
+    rows = full.shape[0] // 8
+    to = device(z, flip(y, odd), flip(x, 1 - odd), c)
+    for r in range(2):
+        first = pl.multiple_of((4 * r + 2 * flip(k, z % 2) + flip(y, step)) * rows, rows)
+        here = full.at[pl.ds(first, rows), :]
+        arrived(here, recv.at[k, step, r])
+        made = remote(here, here, send.at[r, 1, 1], recv.at[k, 1, r], to)
+        made.start()
+        links.sent.append(made)
+
+
+def spread_wait(me, full, recv):
+    z, y, x, c = me
+    odd = flip(c, x)
+    here = full.at[pl.ds(0, full.shape[0] // 8), :]
+    for k, step in ((1 - odd, odd), (odd, 0), (odd, 1)):
+        for r in range(2):
+            arrived(here, recv.at[k, step, r])
+
+
+def join_go(links, me, k, grads, into, relay, send, recv, relay_recv):
+    z, y, x, c = me
+    odd = flip(c, x) == 1
+    even = jnp.logical_not(odd)
+    rows = into.shape[2]
+    for r in range(2):
+
+        def block(step):
+            index = 4 * r + 2 * flip(k, z % 2) + flip(y, step)
+            return grads.at[pl.ds(pl.multiple_of(index * rows, rows), rows), :]
+
+        same, other = device(z, y, c, r), device(z, 1 - y, c, r)
+        mine = jnp.logical_and(even, c == r)
+        partner = jnp.logical_and(even, c != r)
+        links.go_if(
+            partner, mine, block(0), into.at[k, 0], send.at[k, 0, r], recv.at[k, 0], same
+        )
+        if k == 0:
+            links.go_if(even, None, block(1), into.at[0, 1], send.at[0, 1, r], recv.at[0, 1], other)
+            to = device(z, 1 - y, x, c)
+        else:
+            links.go_if(odd, None, block(0), into.at[1, 1], send.at[1, 1, r], recv.at[1, 1], same)
+            to = device(z, y, c, c)
+        links.go_if(odd, None, block(1), relay.at[r], send.at[k, 2, r], relay_recv.at[r], to)
+
+
+def join_relay(links, me, grads, into, relay, send, recv, relay_recv):
+    z, y, x, c = me
+    odd = flip(c, x)
+    k, step = 1 - odd, 1 - odd
+    rows = into.shape[2]
+    for r in range(2):
+        arrived(relay.at[r], relay_recv.at[r])
+        index = 4 * r + 2 * flip(k, z % 2) + flip(y, step)
+        own = grads[pl.ds(pl.multiple_of(index * rows, rows), rows), :]
+        total = relay[r].astype(jnp.float32) + own.astype(jnp.float32)
+        relay[r] = total.astype(jnp.bfloat16)
+        to = device(z, flip(y, step), c, r)
+        made = remote(relay.at[r], into.at[k, 2], send.at[0, 3, r], recv.at[k, 2], to)
+        made.start()
+        links.sent.append(made)
+
+
+def join_sum(k, into, recv):
+    total = 0.0
+    for j in range(3):
+        arrived(into.at[k, j], recv.at[k, j])
+        total = total + into[k, j].astype(jnp.float32)
+    return total.astype(jnp.bfloat16)
+
+
+def rms(rows):
+    return lax.rsqrt(jnp.mean(rows * rows, axis=-1, keepdims=True) + epsilon)
+
+
+def lane_sum(values):
+    return jnp.sum(values, axis=-1, keepdims=True)
+
+
+def head_of(z, y, x, c, heads):
+    return 2 * c + z // 2, (z % 2) * (heads // 2) + 2 * x + y
+
+
+def entry_kernel(
+    lengths, tok_ref, cot_ref, small_ref, bucket_ref, wq_ref, wk_ref, wv_ref, wo_ref, wg_ref,
+    rows_ref, normed, grads, pieces, weight, gain_one, gain_two, rev_ref, slots_o, slots_g,
+    tok_in, cot_in, held, qkv, small, send, recv, plane_send, plane_recv, local,
+):
+    me = z, y, x, c = position()
+    greet(*me)
+    links = Links(send, recv)
+    f, part, half = 2 * x + c, tok_in.shape[2], tok_in.shape[1]
+
+    def gather_rows(n, ref, into):
+        def source(xd, cd):
+            return ref.at[xd, pl.ds(pl.multiple_of(cd * half, half), half)]
+
+        own = pltpu.make_async_copy(source(x, c), into.at[f], local.at[n])
+        own.start()
+        got = []
+        for d in (1, 2, 3):
+            xd, cd = flip(x, d // 2), flip(c, d % 2)
+            got.append(links.go(source(xd, cd), into.at[f], device(z, y, xd, cd)))
+        return own, got
+
+    tok_own, tok_got = gather_rows(0, tok_ref, tok_in)
+    small[f, z, y] = small_ref[...]
+    small_got = []
+    for d in (1, 2, 3):
+        here = small.at[f, z, y]
+        small_got.append(links.go(here, here, device(flip_pair(z, d), y, x, c)))
+    group_width = wq_ref.shape[1] // 2
+    way = []
+    for k in range(2):
+        cut = pl.ds(pl.multiple_of(flip(k, z % 2) * group_width, group_width), group_width)
+        for n, ref in enumerate((wq_ref, wk_ref, wv_ref)):
+            target = held.at[k, :, n * group_width : (n + 1) * group_width]
+            way.append(column_go(links, me, k, ref.at[:, cut], target))
+    cot_own, cot_got = gather_rows(1, cot_ref, cot_in)
+    for made in small_got:
+        made.wait_recv()
+    here = small.at[f, :, y]
+    links.go(here, here, device(z, 1 - y, x, c)).wait_recv()
+    tables = []
+    for d in (1, 2, 3):
+        here = small.at[f]
+        tables.append(links.go(here, here, device(z, y, flip(x, d // 2), flip(c, d % 2))))
+    for i in range(4 * part // BLOCK):
+        here = slice(i * BLOCK, (i + 1) * BLOCK)
+        block = (i // 2) // 2, (i // 2) % 2
+        gain_one[:, here] = small[f, block[0], block[1], i % 2 : i % 2 + 1, :]
+        gain_two[:, here] = small[f, block[0], block[1], 2 + i % 2 : 3 + i % 2, :]
+    tok_own.wait()
+    for made in tok_got:
+        made.wait_recv()
+    wide = [tok_in[i].astype(jnp.float32) for i in range(4)]
+    mean = sum(lane_sum(w * w) for w in wide) / (4 * part)
+    scale = lax.rsqrt(mean + epsilon)
+    for i in range(4):
+        here = slice(i * part, (i + 1) * part)
+        rows_ref[:, here] = tok_in[i]
+        normed[0, :, here] = (wide[i] * scale * gain_one[:, here]).astype(jnp.bfloat16)
+    first = share_start(links, normed, me)
+    cot_own.wait()
+    for made in cot_got:
+        made.wait_recv()
+    slot = (4 * z + 2 * y + c) * half + lax.broadcasted_iota(jnp.int32, (half, part), 0)
+    valid = slot < jnp.where(x == 0, lengths[0], lengths[1])
+    for i in range(4):
+        grads[:, i * part : (i + 1) * part] = jnp.where(valid, cot_in[i], jnp.zeros_like(cot_in[i]))
+    for k in range(2):
+        for made in way[3 * k : 3 * k + 3]:
+            made.wait_recv()
+        spread_go(links, me, k, held.at[k], weight, plane_send, plane_recv)
+    share_step(links, normed, me, first, 1)
+    share_step(links, normed, me, first, 2)
+    later = []
+    half_ffn = wg_ref.shape[1] // 2
+    for k in range(2):
+        side = flip(k, z % 2)
+        cut = pl.ds(pl.multiple_of(side * group_width, group_width), group_width)
+        later.append(column_go(links, me, k, wo_ref.at[:, cut], slots_o.at[k]))
+        cut = pl.ds(pl.multiple_of(side * half_ffn, half_ffn), half_ffn)
+        later.append(column_go(links, me, k, wg_ref.at[:, cut], slots_g.at[k]))
+    spread_relay(links, me, weight, plane_send, plane_recv)
+    for made in tables:
+        made.wait_recv()
+    group = qkv.shape[1]
+    heads = 2 * group
+    source, place = head_of(z, y, x, c, heads)
+    lane = lax.broadcasted_iota(jnp.int32, (1, BLOCK), 1)
+    line = jnp.zeros(bucket_ref.shape, jnp.float32)
+    per_block = 4
+    for n in range(8 * per_block):
+        block = n // per_block
+        row = small[source, block // 2, block % 2, 4:5, :]
+        value = lane_sum(jnp.where(lane == (n % per_block) * heads + place, row, 0.0))
+        line = jnp.where(bucket_ref[...] == n, value, line)
+    rev_ref[...] = line
+    spread_wait(me, weight, plane_recv)
+    rows = normed.shape[1]
+    sent = []
+
+    def project(d):
+        out = jnp.dot(pair_of(normed, d), weight[...], preferred_element_type=jnp.float32)
+        out = out.astype(jnp.bfloat16).T
+        for side, slot in enumerate((d, 4 + d)):
+            here = lanes(slot * rows, rows)
+            cut = out[:, side * rows : (side + 1) * rows]
+            qkv[:, :, :, here] = cut.reshape(3, group, DH, rows)
+            pieces[0, :, :, here] = qkv[:, 2 * x + y, :, here]
+            for e in (1, 2, 3):
+                xd, yd = flip(x, e // 2), flip(y, e % 2)
+                source = qkv.at[:, 2 * xd + yd, :, here]
+                sent.append(links.go(source, pieces.at[e, :, :, here], device(z, yd, xd, c)))
+
+    order = sum_order(z)
+    first[1][0].wait_recv()
+    project(0)
+    for step in (1, 2, 3):
+        if step == 3:
+            share_step(links, normed, me, first, 3)
+        for made in first[1][1 + CHUNKS * (step - 1) : 1 + CHUNKS * step]:
+            made.wait_recv()
+        project(order[step - 1])
+    for made in sent + later:
+        made.wait_recv()
+    links.finish()
+
+
+def low_array(*shape):
+    return jax.ShapeDtypeStruct(shape, jnp.bfloat16)
+
+
+def wide_array(*shape):
+    return jax.ShapeDtypeStruct(shape, jnp.float32)
+
+
+def low_space(*shape):
+    return pltpu.VMEM(shape, jnp.bfloat16)
+
+
+def entry(lengths, tokens_in, cotangent, small, rev_buckets, weights):
+    _, slot_count, part = tokens_in.shape
+    rows, width = slot_count // 2, 4 * part
+    depth, cols = weights[0].shape
+    group = cols // (2 * DH)
+    wide = 3 * cols // 2
+    return pl.pallas_call(
+        entry_kernel,
+        name="entry",
+        out_shape=[
+            low_array(rows, width),
+            low_array(8, rows, width),
+            low_array(rows, width),
+            low_array(4, 3, DH, 8 * rows),
+            low_array(8 * depth, wide),
+            wide_array(1, width),
+            wide_array(1, width),
+            wide_array(*rev_buckets.shape),
+            low_array(2, depth, cols // 2),
+            low_array(2, depth, weights[4].shape[1] // 2),
+        ],
+        in_specs=[pl.BlockSpec(memory_space=pltpu.SMEM)]
+        + [IN_PLACE] * 2
+        + [IN_VMEM] * 2
+        + [IN_PLACE] * 5,
+        out_specs=[IN_VMEM] * 10,
+        scratch_shapes=[
+            low_space(4, rows, part),
+            low_space(4, rows, part),
+            low_space(2, depth, wide),
+            low_space(3, group, DH, 8 * rows),
+            pltpu.VMEM((4, 4, 2, 8, BLOCK), jnp.float32),
+            COPIES((64,)),
+            COPIES((64,)),
+            COPIES((2, 2, 2)),
+            COPIES((2, 2, 2)),
+            COPIES((2,)),
+        ],
+        compiler_params=pltpu.CompilerParams(
+            collective_id=1, has_side_effects=True, vmem_limit_bytes=48 << 20
+        ),
+    )(lengths, tokens_in, cotangent, small, rev_buckets, *weights)
+
+
+def gelu_pair(t):
+    inner = jnp.tanh(root_two_over_pi * (t + 0.044715 * (t * t * t)))
+    half = 0.5 * (1.0 + inner)
+    slope = half + 0.5 * t * (1.0 - inner * inner) * root_two_over_pi * (1.0 + 0.134145 * (t * t))
+    return t * half, slope
+
+
+def pair_of(ref, slot):
+    return jnp.concatenate([ref[slot], ref[4 + slot]], axis=0)
+
+
+def pair_go(links, me, core, i, terms, core_out, core_in):
+    z, y, x, c = me
+    size = terms.shape[0] // 2
+    core_out[i] = terms[size:].astype(jnp.bfloat16)
+    core.append(links.go(core_out.at[i], core_in.at[i], device(z, y, x, 1 - c)))
+    return terms[:size]
+
+
+def sum_step(links, me, core, ring, i, mine, core_in, ring_out, ring_in):
     z, y, x, c = me
     following, _ = ring_of(z)
-    mine = product(sum_order(z)[i])
     rows = mine.shape[0] // CHUNKS
-    core[i].wait_recv()
+    core.wait_recv()
     sent, last = [], []
     for h in range(CHUNKS):
         cut = slice(h * rows, (h + 1) * rows)
@@ -790,231 +1057,17 @@
     return last
 
 
-def column_go(links, me, k, source, target):
-    z, y, x, c = me
-    own = z // 2 == c if k == 0 else None
-    to = device(2 * c + flip(k, z % 2), y, x, z // 2)
-    return links.go_unless(own, source, target, to)
-
-
-def spread_go(links, me, k, source, full, send, recv):
-    z, y, x, c = me
-    rows = source.shape[0]
-    first = pl.multiple_of((4 * c + 2 * flip(k, z % 2) + y) * rows, rows)
-    target = full.at[pl.ds(first, rows), :]
-    for dy in range(2):
-        for dx in range(2):
-            own = None if dy + dx else c == x
-            to = device(z, flip(y, dy), flip(x, dx), x)
-            links.go_unless(own, source, target, to, send.at[k, dy, dx], recv.at[k, dy, c])
-
-
-def spread_wait(full, recv):
-    rows = full.shape[0] // 8
-    for k in range(2):
-        for dy in range(2):
-            for r in range(2):
-                here = full.at[pl.ds(0, rows), :]
-                pltpu.make_async_copy(here, here, recv.at[k, dy, r]).wait()
-
-
-def join_go(links, me, k, grads, into, send, recv):
-    z, y, x, c = me
-    rows = into.shape[3]
-    for dy in range(2):
-        for r in range(2):
-            block = 4 * r + 2 * flip(k, z % 2) + flip(y, dy)
-            source = grads.at[pl.ds(pl.multiple_of(block * rows, rows), rows), :]
-            own = None if dy else jnp.logical_and(c == x, c == r)
-            to = device(z, flip(y, dy), c, r)
-            links.go_unless(
-                own, source, into.at[k, dy, x], to, send.at[k, dy, r], recv.at[k, dy, x]
-            )
-
-
-def join_sum(k, into, recv):
-    total = 0.0
-    for dy in range(2):
-        for other in range(2):
-            here = into.at[k, dy, other]
-            pltpu.make_async_copy(here, here, recv.at[k, dy, other]).wait()
-            total = total + into[k, dy, other].astype(jnp.float32)
-    return total.astype(jnp.bfloat16)
-
-
-def rms(rows):
-    return lax.rsqrt(jnp.mean(rows * rows, axis=-1, keepdims=True) + epsilon)
-
-
-def lane_sum(values):
-    return jnp.sum(values, axis=-1, keepdims=True)
-
-
-def head_of(z, y, x, c, heads):
-    return 2 * c + z // 2, (z % 2) * (heads // 2) + 2 * x + y
-
-
-def entry_kernel(
-    lengths, tok_ref, cot_ref, small_ref, bucket_ref, wq_ref, wk_ref, wv_ref,
-    rows_ref, normed, grads, pieces, weight, gain_one, gain_two, rev_ref,
-    tok_in, cot_in, held, qkv, small, send, recv, plane_send, plane_recv,
-):
-    me = z, y, x, c = position()
-    greet(*me)
-    links = Links(send, recv)
-    f, part, half = 2 * x + c, tok_in.shape[2], tok_in.shape[1]
-
-    def gather_rows(ref, into):
-        got = []
-        for d in (1, 2, 3):
-            xd, cd = flip(x, d // 2), flip(c, d % 2)
-            source = ref.at[xd, pl.ds(pl.multiple_of(cd * half, half), half)]
-            got.append(links.go(source, into.at[f], device(z, y, xd, cd)))
-        into[f] = ref[x, pl.ds(pl.multiple_of(c * half, half), half), :]
-        return got
-
-    tok_got = gather_rows(tok_ref, tok_in)
-    small[f, z, y] = small_ref[...]
-    small_got = []
-    for d in (1, 2, 3):
-        here = small.at[f, z, y]
-        small_got.append(links.go(here, here, device(flip_pair(z, d), y, x, c)))
-    group_width = wq_ref.shape[1] // 2
-    way = []
-    for k in range(2):
-        cut = pl.ds(pl.multiple_of(flip(k, z % 2) * group_width, group_width), group_width)
-        for n, ref in enumerate((wq_ref, wk_ref, wv_ref)):
-            target = held.at[k, :, n * group_width : (n + 1) * group_width]
-            way.append(column_go(links, me, k, ref.at[:, cut], target))
-    cot_got = gather_rows(cot_ref, cot_in)
-    for made in small_got:
-        made.wait_recv()
-    here = small.at[f, :, y]
-    links.go(here, here, device(z, 1 - y, x, c)).wait_recv()
-    tables = []
-    for d in (1, 2, 3):
-        here = small.at[f]
-        tables.append(links.go(here, here, device(z, y, flip(x, d // 2), flip(c, d % 2))))
-    for i in range(4 * part // BLOCK):
-        here = slice(i * BLOCK, (i + 1) * BLOCK)
-        block = (i // 2) // 2, (i // 2) % 2
-        gain_one[:, here] = small[f, block[0], block[1], i % 2 : i % 2 + 1, :]
-        gain_two[:, here] = small[f, block[0], block[1], 2 + i % 2 : 3 + i % 2, :]
-    for made in tok_got:
-        made.wait_recv()
-    wide = [tok_in[i].astype(jnp.float32) for i in range(4)]
-    mean = sum(lane_sum(w * w) for w in wide) / (4 * part)
-    scale = lax.rsqrt(mean + epsilon)
-    for i in range(4):
-        here = slice(i * part, (i + 1) * part)
-        rows_ref[:, here] = tok_in[i]
-        normed[0, :, here] = (wide[i] * scale * gain_one[:, here]).astype(jnp.bfloat16)
-    first = share_start(links, normed, me)
-    for made in cot_got:
-        made.wait_recv()
-    slot = (4 * z + 2 * y + c) * half + lax.broadcasted_iota(jnp.int32, (half, part), 0)
-    valid = slot < jnp.where(x == 0, lengths[0], lengths[1])
-    for i in range(4):
-        grads[0, :, i * part : (i + 1) * part] = jnp.where(valid, cot_in[i], jnp.zeros_like(cot_in[i]))
-    for k in range(2):
-        for made in way[3 * k : 3 * k + 3]:
-            made.wait_recv()
-        spread_go(links, me, k, held.at[k], weight, plane_send, plane_recv)
-    for step in (1, 2, 3):
-        share_step(links, normed, me, first, step)
-    second = share_start(links, grads, me)
-    for made in tables:
-        made.wait_recv()
-    group = qkv.shape[1]
-    heads = 2 * group
-    source, place = head_of(z, y, x, c, heads)
-    lane = lax.broadcasted_iota(jnp.int32, (1, BLOCK), 1)
-    line = jnp.zeros(bucket_ref.shape, jnp.float32)
-    per_block = 4
-    for n in range(8 * per_block):
-        block = n // per_block
-        row = small[source, block // 2, block % 2, 4:5, :]
-        value = lane_sum(jnp.where(lane == (n % per_block) * heads + place, row, 0.0))
-        line = jnp.where(bucket_ref[...] == n, value, line)
-    rev_ref[...] = line
-    share_end(first)
-    spread_wait(weight, plane_recv)
-    count = 2 * normed.shape[1]
-
-    @pl.loop(0, 4)
-    def _(i):
-        left = normed[pl.ds(2 * i, 2)].reshape(count, 4 * part)
-        out = jnp.dot(left, weight[...], preferred_element_type=jnp.float32)
-        out = out.astype(jnp.bfloat16).T
-        qkv[:, :, :, lanes(i * count, count)] = out.reshape(3, group, DH, count)
-
-    sent = []
-    for d in (1, 2, 3):
-        xd, yd = flip(x, d // 2), flip(y, d % 2)
-        sent.append(links.go(qkv.at[:, 2 * xd + yd], pieces.at[d], device(z, yd, xd, c)))
-    pieces[0] = qkv[:, 2 * x + y]
-    for step in (1, 2, 3):
-        share_step(links, grads, me, second, step)
-    share_end(second)
-    for made in sent:
-        made.wait_recv()
-    links.finish()
-
-
-def low_array(*shape):
-    return jax.ShapeDtypeStruct(shape, jnp.bfloat16)
-
-
-def wide_array(*shape):
-    return jax.ShapeDtypeStruct(shape, jnp.float32)
-
-
-def low_space(*shape):
-    return pltpu.VMEM(shape, jnp.bfloat16)
-
-
-def entry(lengths, tokens_in, cotangent, small, rev_buckets, weights):
-    _, slot_count, part = tokens_in.shape
-    rows, width = slot_count // 2, 4 * part
-    depth, cols = weights[0].shape
-    group = cols // (2 * DH)
-    wide = 3 * cols // 2
-    return pl.pallas_call(
-        entry_kernel,
-        name="entry",
-        out_shape=[
-            low_array(rows, width),
-            low_array(8, rows, width),
-            low_array(8, rows, width),
-            low_array(4, 3, DH, 8 * rows),
-            low_array(8 * depth, wide),
-            wide_array(1, width),
-            wide_array(1, width),
-            wide_array(*rev_buckets.shape),
-        ],
-        in_specs=[pl.BlockSpec(memory_space=pltpu.SMEM)] + [IN_VMEM] * 7,
-        out_specs=[IN_VMEM] * 8,
-        scratch_shapes=[
-            low_space(4, rows, part),
-            low_space(4, rows, part),
-            low_space(2, depth, wide),
-            low_space(3, group, DH, 8 * rows),
-            pltpu.VMEM((4, 4, 2, 8, BLOCK), jnp.float32),
-            COPIES((64,)),
-            COPIES((64,)),
-            COPIES((2, 2, 2)),
-            COPIES((2, 2, 2)),
-        ],
-        compiler_params=pltpu.CompilerParams(
-            collective_id=1, has_side_effects=True, vmem_limit_bytes=48 << 20
-        ),
-    )(lengths, tokens_in, cotangent, small, rev_buckets, *weights)
-
-
-def middle_kernel(
-    ctx_ref, rows_ref, gain_ref, slot0, slot1,
-    normed, residual_ref, context, out_weight, gate_up, down,
-    ctx_all, core_out, core_in, ring_out, ring_in, send, recv, plane_send, plane_recv,
+def reduce_pair(links, me, state, i, terms, core_out, core_in, ring_out, ring_in):
+    mine = pair_go(links, me, state[0], i, terms, core_out, core_in)
+    return sum_step(links, me, state[0][i], state[1], i, mine, core_in, ring_out, ring_in)
+
+
+def core_kernel(
+    ctx_ref, rows_ref, gain_ref, own_ref, slots_o, slots_g, slot_ud0, slot_ud1,
+    residual_ref, context, down, hidden, low, wide_ref, part_ref, pieces, in_gu, in_d,
+    out_weight, gate_up, normed, grads, pre, ctx_all, heads_out, grad_gu, grad_d,
+    mine, core_out, core_in, ring_out, ring_in, ring_out2, ring_in2,
+    relay_gu, relay_d, send, recv, plane_send, plane_recv, join_send, join_recv, relay_recv,
 ):
     me = z, y, x, c = position()
     greet(*me)
@@ -1024,38 +1077,178 @@
     for d in (1, 2, 3):
         xd, yd = flip(x, d // 2), flip(y, d % 2)
         heads.append(links.go(ctx_ref.at[d], ctx_all.at[own], device(z, yd, xd, c)))
-    start = 0
-    for n, full in enumerate((out_weight, gate_up, down)):
-        cut = slice(start, start + full.shape[1])
-        start = start + full.shape[1]
-        for k, slot in enumerate((slot0, slot1)):
-            spread_go(links, me, k, slot.at[:, cut], full, plane_send.at[n], plane_recv.at[n])
+    grads[0] = own_ref[...]
+    second = share_start(links, grads, me)
+
+    ffn = down.shape[1]
+    fulls = out_weight, gate_up.at[:, :ffn], gate_up.at[:, ffn:], down
+
+    def weight_go(n):
+        slots = (
+            (slots_o.at[0], slots_o.at[1]),
+            (slots_g.at[0], slots_g.at[1]),
+            (slot_ud0.at[:, :ffn], slot_ud1.at[:, :ffn]),
+            (slot_ud0.at[:, ffn:], slot_ud1.at[:, ffn:]),
+        )[n]
+        for k in range(2):
+            spread_go(links, me, k, slots[k], fulls[n], plane_send.at[n], plane_recv.at[n])
+
+    def weight_relay(n):
+        spread_relay(links, me, fulls[n], plane_send.at[n], plane_recv.at[n])
+
+    def weight_wait(n):
+        spread_wait(me, fulls[n], plane_recv.at[n])
+
+    weight_go(0)
     ctx_all[own] = ctx_ref[0]
     for made in heads:
         made.wait_recv()
     group, size, tokens = ctx_all.shape
+    rows, width = residual_ref.shape
+    depth = gate_up.shape[0] // 8
+    half_tokens = tokens // 2
     context[...] = ctx_all[...].reshape(group * size, tokens).T
-    spread_wait(out_weight, plane_recv.at[0])
-    rows = tokens // 8
-
-    def product(block):
-        return right_transposed(
-            context[pl.ds(pl.multiple_of(block * rows, rows), rows), :], out_weight[...]
+    weight_relay(0)
+    weight_go(1)
+    weight_go(2)
+    weight_wait(0)
+    order = sum_order(z)
+
+    def first_row(block):
+        return pl.multiple_of(block * rows, rows)
+
+    def pair_rows(ref, d):
+        return jnp.concatenate(
+            [ref[pl.ds(first_row(d), rows), :], ref[pl.ds(first_row(4 + d), rows), :]], axis=0
         )
 
-    state = reduce_start(links, me, product, core_out, core_in)
+    state = [], []
     for i in range(4):
-        last = reduce_step(links, me, state, i, product, core_in, ring_out, ring_in)
+        terms = right_transposed(pair_rows(context, order[i]), out_weight[...])
+        last = reduce_pair(links, me, state, i, terms, core_out, core_in, ring_out, ring_in)
+        if i < 3:
+            share_step(links, grads, me, second, i + 1)
+        if i == 1:
+            weight_go(3)
+        if i == 2:
+            weight_relay(1)
+            weight_relay(2)
     residual = rows_ref[...].astype(jnp.float32) + jnp.concatenate(last, axis=0)
     residual_ref[...] = residual
-    gain = gain_ref[...].astype(jnp.float32)
+    gain = gain_ref[...]
     normed[0] = (residual * rms(residual) * gain).astype(jnp.bfloat16)
     shared = share_start(links, normed, me)
+    weight_relay(3)
+    share_end(second)
+    for made in state[0]:
+        links.done(made)
+    ring, terms_go = [], []
+
+    def take_in(i):
+        share_step(links, normed, me, shared, i + 1)
+
+    def feed(i):
+        d = order[i]
+        for made in shared[1][:1] if i == 3 else shared[1][1 + CHUNKS * i : 1 + CHUNKS * (i + 1)]:
+            made.wait_recv()
+        gate_up_pre = jnp.dot(
+            pair_of(normed, d), gate_up[...], preferred_element_type=jnp.float32
+        )
+        activated, slope = gelu_pair(gate_up_pre[:, :ffn])
+        up_pre = gate_up_pre[:, ffn:]
+        made = (activated * up_pre).astype(jnp.bfloat16)
+        hidden[pl.ds(first_row(d), rows), :] = made[:rows]
+        hidden[pl.ds(first_row(4 + d), rows), :] = made[rows:]
+        if i == 0:
+            weight_wait(3)
+        grad_hidden = jnp.dot(pair_of(grads, d), down[...], preferred_element_type=jnp.float32)
+        grad_pre = jnp.concatenate(
+            [
+                (grad_hidden * up_pre * slope).astype(jnp.bfloat16),
+                (grad_hidden * activated).astype(jnp.bfloat16),
+            ],
+            axis=1,
+        )
+        pre[pl.ds(first_row(d), rows), :] = grad_pre[:rows]
+        pre[pl.ds(first_row(4 + d), rows), :] = grad_pre[rows:]
+        terms = right_transposed(grad_pre, gate_up[...])
+        kept = []
+        mine[i] = pair_go(links, me, kept, i, terms, core_out, core_in)
+        return kept[0]
+
+    def pass_on(i, core):
+        return sum_step(links, me, core, ring, i, mine[i], core_in, ring_out2, ring_in2)
+
+    joins = (grad_gu, in_gu, relay_gu), (grad_d, in_d, relay_d)
+
+    def weight_grads(k):
+        for n in range(4):
+            block = 4 * (n // 2) + 2 * flip(k, z % 2) + n % 2
+            here = pl.ds(pl.multiple_of(block * depth, depth), depth)
+            left = normed[:, :, here].reshape(tokens, depth)
+            grad_gu[here, :] = left_transposed(left, pre[...]).astype(jnp.bfloat16)
+            left = grads[:, :, here].reshape(tokens, depth)
+            grad_d[here, :] = left_transposed(left, hidden[...]).astype(jnp.bfloat16)
+        for n, (grad, into, relay) in enumerate(joins):
+            sems = join_send.at[n], join_recv.at[n], relay_recv.at[n]
+            join_go(links, me, k, grad, into, relay, *sems)
+
+    take_in(0)
+    weight_wait(1)
+    weight_wait(2)
+    first = feed(0)
+    pass_on(0, first)
+    take_in(1)
+    following = feed(1)
+    take_in(2)
+    final = feed(3)
+    pass_on(1, following)
+    third = feed(2)
+    weight_grads(0)
+    pass_on(2, third)
+    weight_grads(1)
+    last = pass_on(3, final)
+    normed_grad = jnp.concatenate(last, axis=0)
+    residual = residual_ref[...]
+    scale = rms(residual)
+    unit = residual * scale
+    part_ref[...] = jnp.sum(normed_grad * unit, axis=0, keepdims=True)
+    out = own_ref[...].astype(jnp.float32) + norm_back(normed_grad, unit, scale, gain)
+    wide_ref[...] = out
+    low[0] = out.astype(jnp.bfloat16)
+    shared = share_start(links, low, me)
+    sent = []
+
+    def context_back(d):
+        made = jnp.dot(pair_of(low, d), out_weight[...], preferred_element_type=jnp.float32)
+        made = made.astype(jnp.bfloat16).T
+        for half, slot in enumerate((d, 4 + d)):
+            here = lanes(slot * rows, rows)
+            cut = made[:, half * rows : (half + 1) * rows]
+            heads_out[:, :, here] = cut.reshape(group, size, rows)
+            pieces[0, :, here] = heads_out[own, :, here]
+            for e in (1, 2, 3):
+                xd, yd = flip(x, e // 2), flip(y, e % 2)
+                source = heads_out.at[2 * xd + yd, :, here]
+                sent.append(links.go(source, pieces.at[e, :, here], device(z, yd, xd, c)))
+
+    shared[1][0].wait_recv()
+    context_back(0)
     for step in (1, 2, 3):
-        share_step(links, normed, me, shared, step)
-    share_end(shared)
-    spread_wait(gate_up, plane_recv.at[1])
-    spread_wait(down, plane_recv.at[2])
+        share_step(links, low, me, shared, step)
+        if step == 2:
+            for n, (grad, into, relay) in enumerate(joins):
+                sems = join_send.at[n], join_recv.at[n], relay_recv.at[n]
+                join_relay(links, me, grad, into, relay, *sems)
+        for made in shared[1][1 + CHUNKS * (step - 1) : 1 + CHUNKS * step]:
+            made.wait_recv()
+        context_back(order[step - 1])
+    for made in sent:
+        made.wait_recv()
+    for n, (_, into, _) in enumerate(joins):
+        for k in range(2):
+            for j in range(3):
+                arrived(into.at[k, j], join_recv.at[n, k, j])
     links.finish()
 
 
@@ -1068,120 +1261,56 @@
     ]
 
 
-def middle(ctx_pieces, token_rows, gain, slots, widths):
+def core(ctx_pieces, token_rows, gain, grad_own, slots_o, slots_g, slots_ud):
     _, size, tokens = ctx_pieces.shape
     rows, width = token_rows.shape
-    depth = slots[0].shape[0]
+    _, depth, ffn = slots_g.shape
+    group = slots_o.shape[2] // DH
     return pl.pallas_call(
-        middle_kernel,
-        name="middle",
+        core_kernel,
+        name="core",
         out_shape=[
-            low_array(8, rows, width),
             wide_array(rows, width),
             low_array(tokens, 4 * size),
-            *(low_array(8 * depth, w) for w in widths),
-        ],
-        in_specs=[IN_VMEM] * 5,
-        out_specs=[IN_VMEM] * 4 + [IN_PLACE] * 2,
-        scratch_shapes=[
-            low_space(4, size, tokens),
-            *reduce_space(rows, width),
-            COPIES((48,)),
-            COPIES((48,)),
-            COPIES((3, 2, 2, 2)),
-            COPIES((3, 2, 2, 2)),
-        ],
-        compiler_params=pltpu.CompilerParams(
-            collective_id=2, has_side_effects=True, vmem_limit_bytes=48 << 20
-        ),
-    )(ctx_pieces, token_rows, gain, *slots)
-
-
-def back_kernel(
-    pre_ref, weight_ref, residual_ref, own_ref, gain_ref, out_weight, grad_gu, grad_d,
-    low_ref, wide_ref, part_ref, pieces, sum0, sum1,
-    heads_out, in_gu, in_d, core_out, core_in, ring_out, ring_in, send, recv, plane_send, plane_recv,
-):
-    me = z, y, x, c = position()
-    greet(*me)
-    links = Links(send, recv)
-    rows = residual_ref.shape[0]
-
-    def product(block):
-        return right_transposed(
-            pre_ref[pl.ds(pl.multiple_of(block * rows, rows), rows), :], weight_ref[...]
-        )
-
-    for k in range(2):
-        join_go(links, me, k, grad_gu, in_gu, plane_send.at[0], plane_recv.at[0])
-        join_go(links, me, k, grad_d, in_d, plane_send.at[1], plane_recv.at[1])
-    state = reduce_start(links, me, product, core_out, core_in)
-    for i in range(4):
-        last = reduce_step(links, me, state, i, product, core_in, ring_out, ring_in)
-    normed_grad = jnp.concatenate(last, axis=0)
-    residual = residual_ref[...]
-    scale = rms(residual)
-    unit = residual * scale
-    part_ref[...] = jnp.sum(normed_grad * unit, axis=0, keepdims=True)
-    out = own_ref[...].astype(jnp.float32) + norm_back(normed_grad, unit, scale, gain_ref[...])
-    wide_ref[...] = out
-    low_ref[0] = out.astype(jnp.bfloat16)
-    shared = share_start(links, low_ref, me)
-    for step in (1, 2, 3):
-        share_step(links, low_ref, me, shared, step)
-    share_end(shared)
-    group, size, tokens = heads_out.shape
-    count = 2 * rows
-    for i in range(4):
-        left = low_ref[2 * i : 2 * i + 2].reshape(count, low_ref.shape[2])
-        out = jnp.dot(left, out_weight[...], preferred_element_type=jnp.float32)
-        out = out.astype(jnp.bfloat16).T
-        heads_out[:, :, i * count : (i + 1) * count] = out.reshape(group, size, count)
-    heads = []
-    for d in (1, 2, 3):
-        xd, yd = flip(x, d // 2), flip(y, d % 2)
-        heads.append(links.go(heads_out.at[2 * xd + yd], pieces.at[d], device(z, yd, xd, c)))
-    pieces[0] = heads_out[2 * x + y]
-    for made in heads:
-        made.wait_recv()
-    for k in range(2):
-        wide = in_gu.shape[-1]
-        (sum0, sum1)[k][:, :wide] = join_sum(k, in_gu, plane_recv.at[0])
-        (sum0, sum1)[k][:, wide:] = join_sum(k, in_d, plane_recv.at[1])
-    links.finish()
-
-
-def back(grad_pre, gate_up, residual, grad_own, gain, out_weight, grad_gate_up, grad_down):
-    rows, width = residual.shape
-    group = out_weight.shape[1] // DH
-    depth = gate_up.shape[0] // 8
-    return pl.pallas_call(
-        back_kernel,
-        name="back",
-        out_shape=[
+            low_array(8 * depth, ffn),
+            low_array(tokens, ffn),
             low_array(8, rows, width),
             wide_array(rows, width),
             wide_array(1, width),
-            low_array(group, DH, 8 * rows),
-            low_array(depth, grad_gate_up.shape[1] + grad_down.shape[1]),
-            low_array(depth, grad_gate_up.shape[1] + grad_down.shape[1]),
+            low_array(4, size, tokens),
+            low_array(2, 3, depth, 2 * ffn),
+            low_array(2, 3, depth, ffn),
         ],
-        in_specs=[IN_VMEM] * 6 + [IN_PLACE] * 2,
-        out_specs=[IN_VMEM] * 6,
+        in_specs=[IN_VMEM] * 4 + [IN_PLACE] * 4,
+        out_specs=[IN_VMEM] * 8 + [IN_PLACE] * 2,
         scratch_shapes=[
-            low_space(group, DH, 8 * rows),
-            low_space(2, 2, 2, depth, grad_gate_up.shape[1]),
-            low_space(2, 2, 2, depth, grad_down.shape[1]),
+            low_space(8 * depth, group * size),
+            low_space(8 * depth, 2 * ffn),
+            low_space(8, rows, width),
+            low_space(8, rows, width),
+            low_space(tokens, 2 * ffn),
+            low_space(4, size, tokens),
+            low_space(group, size, tokens),
+            low_space(8 * depth, 2 * ffn),
+            low_space(8 * depth, ffn),
+            pltpu.VMEM((4, rows, width), jnp.float32),
             *reduce_space(rows, width),
-            COPIES((48,)),
-            COPIES((48,)),
-            COPIES((2, 2, 2, 2)),
-            COPIES((2, 2, 2, 2)),
+            low_space(3, rows, width),
+            low_space(3, rows, width),
+            low_space(2, depth, 2 * ffn),
+            low_space(2, depth, ffn),
+            COPIES((112,)),
+            COPIES((112,)),
+            COPIES((4, 2, 2, 2)),
+            COPIES((4, 2, 2, 2)),
+            COPIES((2, 2, 4, 2)),
+            COPIES((2, 2, 3)),
+            COPIES((2, 2)),
         ],
         compiler_params=pltpu.CompilerParams(
-            collective_id=3, has_side_effects=True, vmem_limit_bytes=56 << 20
+            collective_id=2, has_side_effects=True, vmem_limit_bytes=63 << 20
         ),
-    )(grad_pre, gate_up, residual, grad_own, gain, out_weight, grad_gate_up, grad_down)
+    )(ctx_pieces, token_rows, gain, grad_own, slots_o, slots_g, *slots_ud)
 
 
 def exit_kernel(
@@ -1191,7 +1320,7 @@
     heads_in, rows_low, grad_qkv, grad_out, in_qkv, in_out, held, token_out, layer_own,
     packed, in_f, in_y, in_z,
     core_out, core_in, ring_out, ring_in, core_out2, core_in2, ring_out2, ring_in2,
-    send, recv, plane_send, plane_recv,
+    relay_qkv, relay_out, send, recv, plane_send, plane_recv, relay_recv,
 ):
     me = z, y, x, c = position()
     greet(*me)
@@ -1208,14 +1337,12 @@
         heads.append(links.go(piece_ref.at[d], heads_in.at[own], device(z, yd, xd, c)))
     heads_in[own] = piece_ref[0]
 
-    def block_rows(ref, block):
-        return ref[pl.ds(pl.multiple_of(block * rows, rows), rows), :]
-
-    def ffn_product(block):
-        return right_transposed(block_rows(hidden_ref, block), down_ref[...])
-
-    def product(block):
-        return right_transposed(block_rows(rows_low, block), weight_ref[...])
+    order = sum_order(z)
+
+    def pair_rows(ref, d):
+        return jnp.concatenate(
+            [ref[lanes(block * rows, rows), :] for block in (d, 4 + d)], axis=0
+        )
 
     def to_home(source, into):
         got = []
@@ -1225,42 +1352,60 @@
         into[f] = source[f]
         return got
 
+    ffn, state = ([], []), ([], [])
+    joins = (grad_qkv, in_qkv, relay_qkv), (grad_out, in_out, relay_out)
+
+    def sems(n):
+        return plane_send.at[n], plane_recv.at[n], relay_recv.at[n]
+
     def ffn_step(i):
-        return reduce_step(links, me, ffn, i, ffn_product, core_in2, ring_out2, ring_in2)
+        terms = right_transposed(pair_rows(hidden_ref, order[i]), down_ref[...])
+        return reduce_pair(links, me, ffn, i, terms, core_out2, core_in2, ring_out2, ring_in2)
 
     def step(i):
-        return reduce_step(links, me, state, i, product, core_in, ring_out, ring_in)
-
-    ffn = reduce_start(links, me, ffn_product, core_out2, core_in2)
+        terms = right_transposed(pair_rows(rows_low, order[i]), weight_ref[...])
+        return reduce_pair(links, me, state, i, terms, core_out, core_in, ring_out, ring_in)
+
+    def weight_grads(k, ref, right, join, n):
+        for part_of_rows in range(4):
+            block = 4 * (part_of_rows // 2) + 2 * flip(k, z % 2) + part_of_rows % 2
+            here = pl.ds(pl.multiple_of(block * depth, depth), depth)
+            left = ref[:, :, here].reshape(tokens, depth)
+            join[0][here, :] = left_transposed(left, right[...]).astype(jnp.bfloat16)
+        join_go(links, me, k, *join, *sems(n))
+
     ffn_step(0)
     for k in range(2):
-        for n in range(4):
-            block = 4 * (n // 2) + 2 * flip(k, z % 2) + n % 2
-            here = pl.ds(pl.multiple_of(block * depth, depth), depth)
-            left = low_ref[:, :, here].reshape(tokens, depth)
-            grad_out[here, :] = left_transposed(left, context_ref[...]).astype(jnp.bfloat16)
-        join_go(links, me, k, grad_out, in_out, plane_send.at[1], plane_recv.at[1])
+        weight_grads(k, low_ref, context_ref, joins[1], 1)
     for made in heads:
         made.wait_recv()
     for n in range(three):
         here = slice(n * group * size, (n + 1) * group * size)
         rows_low[:, here] = heads_in[:, n].reshape(group * size, tokens).T
-    state = reduce_start(links, me, product, core_out, core_in)
     step(0)
     ffn_step(1)
     for k in range(2):
-        for n in range(4):
-            block = 4 * (n // 2) + 2 * flip(k, z % 2) + n % 2
-            here = pl.ds(pl.multiple_of(block * depth, depth), depth)
-            left = normed_ref[:, :, here].reshape(tokens, depth)
-            grad_qkv[here, :] = left_transposed(left, rows_low[...]).astype(jnp.bfloat16)
-        join_go(links, me, k, grad_qkv, in_qkv, plane_send.at[0], plane_recv.at[0])
-        step(1 + k)
-        last = ffn_step(2 + k)
+        weight_grads(k, normed_ref, rows_low, joins[0], 0)
+    join_relay(links, me, *joins[1], *sems(1))
+    step(1)
+    ffn_step(2)
+    join_relay(links, me, *joins[0], *sems(0))
+    step(2)
+    last = ffn_step(3)
     layer = (residual_ref[...] + jnp.concatenate(last, axis=0)).astype(jnp.bfloat16)
     for i in range(4):
         layer_own[i] = layer[:, i * part : (i + 1) * part]
     home = to_home(layer_own, layer_ref)
+    wide_qkv = in_qkv.shape[-1]
+    group_width = wide_qkv // 3
+    cut = pl.ds(pl.multiple_of((z % 2) * group_width, group_width), group_width)
+    way = []
+    for k in range(2):
+        held[k, :, :wide_qkv] = join_sum(k, in_qkv, plane_recv.at[0])
+        held[k, :, wide_qkv:] = join_sum(k, in_out, plane_recv.at[1])
+        for n, ref in enumerate((query_out, key_out, value_out, output_out)):
+            sent = held.at[k, :, n * group_width : (n + 1) * group_width]
+            way.append(column_go(links, me, k, sent, ref.at[:, cut]))
 
     packed[...] = jnp.zeros_like(packed)
     per_block = 4
@@ -1293,16 +1438,6 @@
     for d in (1, 2, 3):
         to = device(z, y, flip(x, d // 2), flip(c, d % 2))
         got.append(links.go(packed, in_f.at[d - 1], to))
-    wide_qkv = in_qkv.shape[-1]
-    group_width = wide_qkv // 3
-    cut = pl.ds(pl.multiple_of((z % 2) * group_width, group_width), group_width)
-    way = []
-    for k in range(2):
-        held[k, :, :wide_qkv] = join_sum(k, in_qkv, plane_recv.at[0])
-        held[k, :, wide_qkv:] = join_sum(k, in_out, plane_recv.at[1])
-        for n, ref in enumerate((query_out, key_out, value_out, output_out)):
-            sent = held.at[k, :, n * group_width : (n + 1) * group_width]
-            way.append(column_go(links, me, k, sent, ref.at[:, cut]))
     for made in got:
         made.wait_recv()
     for made in got:
@@ -1347,8 +1482,8 @@
             low_space(tokens, wide),
             low_space(8 * depth, wide),
             low_space(8 * depth, out_wide),
-            low_space(2, 2, 2, depth, wide),
-            low_space(2, 2, 2, depth, out_wide),
+            low_space(2, 3, depth, wide),
+            low_space(2, 3, depth, out_wide),
             low_space(2, depth, wide + out_wide),
             low_space(4, rows, width // 4),
             low_space(4, rows, width // 4),
@@ -1358,16 +1493,47 @@
             pltpu.VMEM((3, *tile), jnp.float32),
             *reduce_space(rows, width),
             *reduce_space(rows, width),
+            low_space(2, depth, wide),
+            low_space(2, depth, out_wide),
             COPIES((64,)),
             COPIES((64,)),
-            COPIES((2, 2, 2, 2)),
-            COPIES((2, 2, 2, 2)),
+            COPIES((2, 2, 4, 2)),
+            COPIES((2, 2, 3)),
+            COPIES((2, 2)),
         ],
         compiler_params=pltpu.CompilerParams(
             collective_id=4, has_side_effects=True, vmem_limit_bytes=60 << 20
         ),
     )(pieces, normed, weight, token_rows, wide_grad, gain, low, context, hidden, down, residual,
       gain_two_part, line_grad, rev_buckets)
+
+
+def widen_kernel(*refs):
+    attn, slots, home, outs = refs[:4], refs[4:6], refs[6], refs[7:]
+    z_low = (lax.axis_index("seq") // 2) % 2
+    for ref, out in zip(attn, outs[:4]):
+        out[...] = ref[...].astype(jnp.float32)
+    size = slots[0].shape[1] // 3
+    for k in range(2):
+        cut = lanes((k + z_low - 2 * k * z_low) * size, size)
+        for n, out in enumerate(outs[4:7]):
+            out[:, cut] = slots[k][:, n * size : (n + 1) * size].astype(jnp.float32)
+    outs[7][...] = home[...].astype(jnp.float32)
+
+
+def widen(attn, slots, home):
+    depth, cols = attn[0].shape
+    size = 2 * slots[0].shape[1] // 3
+    return pl.pallas_call(
+        widen_kernel,
+        name="widen",
+        out_shape=[wide_array(depth, cols)] * 4
+        + [wide_array(depth, size)] * 3
+        + [wide_array(*home.shape)],
+        in_specs=[IN_VMEM] * 7,
+        out_specs=[IN_VMEM] * 8,
+        compiler_params=pltpu.CompilerParams(vmem_limit_bytes=32 << 20),
+    )(*attn, *slots, home)
 
 
 def fast_shards(
@@ -1416,43 +1582,49 @@
     )
     small = small.astype(jnp.float32).reshape(8, BLOCK)
     rev_buckets = jnp.concatenate([buckets[::-1], jnp.full((1,), -1, jnp.int32)])[None, :]
-    token_low, normed_one, grad_rows, pieces, qkv_weight, gain_one, gain_two, rev_line = entry(
+    (
+        token_low,
+        normed_one,
+        grad_own,
+        pieces,
+        qkv_weight,
+        gain_one,
+        gain_two,
+        rev_line,
+        slots_o,
+        slots_g,
+    ) = entry(
         lengths,
         tokens_in,
         cotangent,
         small,
         rev_buckets,
-        (query_weight, key_weight, value_weight),
-    )
-    tokens = 4 * slot_count
-    grad_own = grad_rows[0]
-    later = halves([output_weight, gate_weight, up_weight, down_weight])
-    pieces, *later = lax.optimization_barrier((pieces, *later))
-    held = [move(later[k], spread_slot(k)) for k in range(2)]
+        (query_weight, key_weight, value_weight, output_weight, gate_weight),
+    )
+    pieces, *later = lax.optimization_barrier((pieces, *halves([up_weight, down_weight])))
+    slots_ud = [move(later[k], spread_slot(k)) for k in range(2)]
     context_pieces, context_wide, lse, qkv_all = attend(lengths, pieces, rev_line)
-    normed_two, residual, context, output_full, gate_up, down_full = middle(
-        context_pieces, token_low, gain_two, held, (group_width, 2 * hidden_width, hidden_width)
-    )
-    normed_two = normed_two.reshape(tokens, width)
-    grad_rows = grad_rows.reshape(tokens, width)
-    gate_up_pre = plain_product(normed_two, gate_up)
-    gate_pre, up_pre = gate_up_pre[:, :hidden_width], gate_up_pre[:, hidden_width:]
-    activated, gelu_back = jax.vjp(jax.nn.gelu, gate_pre)
-    hidden = (activated * up_pre).astype(jnp.bfloat16)
-    grad_hidden = plain_product(grad_rows, down_full)
-    grad_pre = jnp.concatenate(
-        [
-            gelu_back(grad_hidden * up_pre)[0].astype(jnp.bfloat16),
-            (grad_hidden * activated).astype(jnp.bfloat16),
-        ],
-        axis=1,
-    )
-    grad_gate_up = left_transposed(normed_two, grad_pre).astype(jnp.bfloat16)
-    grad_down = left_transposed(grad_rows, hidden).astype(jnp.bfloat16)
-    residual_low, residual_grad, gain_two_part, grad_pieces, *sums = back(
-        grad_pre, gate_up, residual, grad_own, gain_two, output_full, grad_gate_up, grad_down
-    )
-    ffn_slots = [move(sums[k], spread_slot(k)) for k in range(2)]
+    (
+        residual,
+        context,
+        down_full,
+        hidden,
+        residual_low,
+        residual_grad,
+        gain_two_part,
+        grad_pieces,
+        terms_gate_up,
+        terms_down,
+    ) = core(context_pieces, token_low, gain_two, grad_own, slots_o, slots_g, slots_ud)
+
+    def slot_sum(k):
+        sums = [
+            jnp.sum(t[k].astype(jnp.float32), axis=0).astype(jnp.bfloat16)
+            for t in (terms_gate_up, terms_down)
+        ]
+        return jnp.concatenate(sums, axis=1)
+
+    ffn_slots = [move(slot_sum(k), spread_slot(k)) for k in range(2)]
     qkv_grad_pieces, line_grad = attend_back(
         lengths, grad_pieces, rev_line, context_wide, lse, qkv_all
     )
@@ -1473,17 +1645,11 @@
         line_grad,
         rev_buckets,
     )
-    token_share = home.astype(jnp.float32).reshape(batch_count, slot_count, part_width)
+    query_sum, key_sum, value_sum, output_sum, gate_sum, up_sum, down_sum, home = widen(
+        attn_sums, ffn_slots, home
+    )
+    token_share = home.reshape(batch_count, slot_count, part_width)
     layer_out = layer.reshape(batch_count, slot_count, part_width)
-
-    def own_columns(first, size):
-        cut = [s[:, first : first + size].astype(jnp.float32) for s in ffn_slots]
-        return jnp.concatenate(
-            [jnp.where(z_low == 0, cut[0], cut[1]), jnp.where(z_low == 0, cut[1], cut[0])], axis=1
-        )
-
-    query_sum, key_sum, value_sum, output_sum = (s.astype(jnp.float32) for s in attn_sums)
-    gate_sum, up_sum, down_sum = (own_columns(i * hidden_width, hidden_width) for i in range(3))
     table_sum = lax.dynamic_slice_in_dim(
         small[4].reshape(-1, 4 * heads), fsdp_index * heads, heads, 1
     )

time: 603 us -> 552 us (0.915); the launches traced: 604 us -> 544 us
  Pallas kernels: 539 us -> 505 us
  matrix products: 28.3 us -> 0 us
  other arithmetic: 15.2 us -> 6.03 us
  local copies, waits for them, and re-layouts: 15.3 us -> 24.2 us
    pallas_call x1, Pallas kernels: 49.8 us -> 15 us  [attend(): pl.pallas_call(attend_kernel, name='attend', out_shape=[jax.ShapeDtypeStr...]
    dot_general x4 -> x0, matrix products: 28.3 us -> none  [the longest x2 15.6 us: plain_product(): return jnp.dot(left, right, preferred_element_type=jnp.float32)]
    pallas_call x1, Pallas kernels: 48.2 us -> 22.7 us  [attend_back(): pl.pallas_call(attend_back_kernel, name='attend_back', out_shape=[jax.Sha...]
    pallas_call x2, Pallas kernels: 218 us -> 241 us  [the longest x1 238 us: core(): pl.pallas_call(core_kernel, name='core', out_shape=[wide_array(rows, widt...]
    pallas_call x1, Pallas kernels: 123 us -> 136 us  [leave(): pl.pallas_call(exit_kernel, name='leave', out_shape=[*(low_array(depth, c...]
    unnamed x63 -> x71, local copies, waits for them, and re-layouts: 7.29 us -> 19.3 us
    pallas_call x1, Pallas kernels: 99.8 us -> 89.1 us  [entry(): pl.pallas_call(entry_kernel, name='entry', out_shape=[low_array(rows, wid...]
  transfers between devices with their start and end apart: 4 -> 4, of which waited for: 0 -> 1; matrix products, arithmetic and copies ran while one was open for 0% -> 0% of each run, Pallas kernels for 16% -> 7%
where the time goes in v1:
time: 552 us; the launch traced here: 544 us
  Pallas kernels  505 us (91%)
  local copies, waits for them, and re-layouts  24.2 us (4%)
  other arithmetic  6.03 us (1%)
    pallas_call x1, Pallas kernels, core(): pl.pallas_call(core_kernel, name='core', out_shape=[wide_array(rows, widt...  238 us
    pallas_call x1, Pallas kernels, leave(): pl.pallas_call(exit_kernel, name='leave', out_shape=[*(low_array(depth, c...  136 us
    pallas_call x1, Pallas kernels, entry(): pl.pallas_call(entry_kernel, name='entry', out_shape=[low_array(rows, wid...  89.1 us
    pallas_call x1, Pallas kernels, attend_back(): pl.pallas_call(attend_back_kernel, name='attend_back', out_shape=[jax.Sha...  22.7 us
    unnamed x71, local copies, waits for them, and re-layouts  19.3 us
    pallas_call x1, Pallas kernels, attend(): pl.pallas_call(attend_kernel, name='attend', out_shape=[jax.ShapeDtypeStr...  15 us
  transfers between devices with their start and end apart: 4, of which 1 were waited for; matrix products, arithmetic and copies ran while one was open for 0% of the time, Pallas kernels for 7%

profile of v1, /device:TPU:0, one launch (start us, length us, event | category | flops | bytes accessed | tf_op | source)
XLA Modules:
  0.0 543.9 jit_solution(11720492762243354360)
XLA Ops:
  0.7 0.8 reshape.43
  1.4 0.8 reverse
  2.2 0.1 slice.35
  2.3 0.1 pad_add_fusion
  2.4 1.4 constant_dynamic-slice_fusion.1
  4.1 0.4 copy-done.32
  4.5 0.1 fusion.small_ref
  4.6 0.4 copy-done.2
  4.9 0.2 copy-done.5
  5.1 0.2 copy-done.6
  5.3 0.1 copy-done.10
  5.4 0.1 copy-done.11
  5.5 89.1 %entry.1 = (bf16[128,2048]{1,0:T(8,128)(2,1)S(1)}, bf16[8,128,2048]{2,1,0:T(8,128)(2,1)}, bf16[128,2048]{1,0:T(8,128)(2,1)S(1)}, bf16[4,3,64,1024]{3,2,1,0:T(8,1...) custom-call(s32[2]{0:T(128)S(1)} %copy-done.22, ...), custom_call_target="tpu_custom_call" | custom-call | tf_op jit(solution)/shard_map/entry/pallas_call | solution.py:980
  94.6 0.8 copy-done
  95.4 0.8 copy-done.3
  96.3 0.8 copy-done.7
  97.0 0.7 copy-done.17
  97.7 0.6 copy-done.20
  98.3 0.6 copy-done.21
  98.9 0.7 collective-permute-start
  99.7 1.4 copy-done.23
  101.1 15.0 %attend.1 = (bf16[4,64,1024]{2,1,0:T(8,128)(2,1)S(1)}, f32[2,64,2048]{2,1,0:T(8,128)S(1)}, f32[2,1,2048]{2,1,0:T(1,128)S(1)}, bf16[2,3,64,2048]{3,2,1,0:T(8,128)(2,1)S(1)}) custom-call(s32[2]{0:T(128)S(1)} %copy-done.22, bf16[4,3,64,1024]{3,2,1,0:T(8,128)(2,1)S(1)} %copy-done.23, f32[1,4096]{1,0:T(1,128)S(1)} %get-tuple-element.61.rev_ref), custom_call_target="tpu_custom_call" | custom-call | flops 46000001024 | bytes 4194304 | tf_op jit(solution)/shard_map/attend/pallas_call | solution.py:438
  116.1 0.8 copy-done.8
  116.9 1.1 copy-done.25
  118.1 1.0 copy-done.27
  119.0 5.3 collective-permute-done.1.slot_ud1
  124.3 0.8 copy-done.30
  125.2 238.1 %core.1 = (f32[128,2048]{1,0:T(8,128)}, bf16[1024,256]{1,0:T(8,128)(2,1)}, bf16[2048,640]{1,0:T(8,128)(2,1)}, bf16[1024,640]{1,0:T(8,128)(2,1)}, bf16[8,128,2048...) custom-call(bf16[4,64,1024]{2,1,0:T(8,128)(2,1)} %copy-done.8, ...), custom_call_target="tpu_custom_call" | custom-call | tf_op jit(solution)/shard_map/core/pallas_call | solution.py:1269
  363.3 2.1 slice_reduce_fusion.2
  365.4 3.5 slice_reduce_fusion
  369.0 0.9 collective-permute-start.2
  370.0 0.6 collective-permute-start.3
  370.6 0.2 copy-done.28
  370.8 22.7 %attend_back.1 = (bf16[4,3,64,1024]{3,2,1,0:T(8,128)(2,1)S(1)}, f32[1,4096]{1,0:T(1,128)S(1)}) custom-call(s32[2]{0:T(128)S(1)} %copy-done.22, bf16[4,64,1024]{2,1,0:T(8,128)(2,1)S(1)} %copy-done.24, f32[1,4096]{1,0:T(1,128)S(1)} %get-tuple-element.61.rev_ref, f32[2,64,2048]{2,1,0:T(8,128)S(1)} %copy-done.28, f32[2,1,2048]{2,1,0:T(1,128)S(1)} %get-tuple-element.72.lse_ref, ...), custom_call_target="tpu_custom_call" | custom-call | flops 46000001024 | bytes 4194304 | tf_op jit(solution)/shard_map/attend_back/pallas_call | solution.py:559
  393.5 1.2 copy-done.1
  394.7 0.6 copy-done.19
  395.3 136.5 %leave.1 = (bf16[256,512]{1,0:T(8,128)(2,1)}, bf16[256,512]{1,0:T(8,128)(2,1)}, bf16[256,512]{1,0:T(8,128)(2,1)}, bf16[256,512]{1,0:T(8,128)(2,1)}, bf16[4,128,5...) custom-call(bf16[4,3,64,1024]{3,2,1,0:T(8,128)(2,1)} %copy-done.1, ...), custom_call_target="tpu_custom_call" | custom-call | tf_op jit(solution)/shard_map/leave/pallas_call | solution.py:1469
  531.8 0.7 slice_reduce_fusion.4
  532.5 1.3 slice_bitcast_fusion
  533.8 0.1 reshape_squeeze.3
  533.9 0.7 constant_dynamic-slice_fusion
  534.5 1.0 copy-done.4
  535.6 0.9 copy-done.13
  536.5 0.9 copy-done.14
  537.5 0.9 copy-done.15
  538.4 0.9 copy-done.16
  539.4 3.2 widen.1
  542.6 0.8 copy.27
  (52 shorter events, 0.5 us)
Async XLA Ops:
  2.4 2.2 copy-start.18
  2.4 2.2 copy-start.12
  3.8 0.7 copy-start.32
  3.8 0.7 copy-start.33
  3.8 1.1 copy-start.2
  3.9 1.2 copy-start.5
  3.9 1.4 copy-start.6
  3.9 1.4 copy-start.9
  3.9 1.5 copy-start.10
  3.9 1.6 copy-start.11
  3.9 1.6 copy-start.22
  94.6 0.8 copy-start
  95.4 0.8 copy-start.3
  96.3 0.8 copy-start.7
  97.0 0.7 copy-start.17
  97.7 0.6 copy-start.20
  98.3 0.6 copy-start.21
  98.9 20.1 %collective-permute-start = (bf16[256,1280]{1,0:T(8,128)(2,1)S(1)}, bf16[256,1280]{1,0:T(8,128)(2,1)S(1)}, u32[]{:S(2)}, u32[]{:S(2)}) collective-permute-start(bf16[256,1280]{1,0:T(8,128)(2,1)S(1)} %pad_maximum_fusion.2), channel_id=1, source_target_pairs={{0,0},{1,16},{2,2},{3,18},{4,4},{5,20},{6,6},{7,22},{8,8},{9,24},{... | collective-permute-start | bytes 1966088 | tf_op jit(solution)/shard_map/ppermute | solution.py:327
  99.6 24.7 %collective-permute-start.1 = (bf16[256,1280]{1,0:T(8,128)(2,1)S(1)}, bf16[256,1280]{1,0:T(8,128)(2,1)S(1)}, u32[]{:S(2)}, u32[]{:S(2)}) collective-permute-start(bf16[256,1280]{1,0:T(8,128)(2,1)S(1)} %pad_maximum_fusion.3), channel_id=1, source_target_pairs={{0,8},{1,24},{2,10},{3,26},{4,12},{5,28},{6,14},{7,30},{8,0},{9,16... | collective-permute-start | bytes 1966088 | tf_op jit(solution)/shard_map/ppermute | solution.py:327
  99.7 1.4 copy-start.23
  116.1 0.8 copy-start.8
  116.9 1.1 copy-start.25
  118.1 1.0 copy-start.27
  119.0 6.1 %copy-start.29 = (bf16[256,1280]{1,0:T(8,128)(2,1)}, bf16[256,1280]{1,0:T(8,128)(2,1)S(1)}, u32[]{:S(2)}) copy-start(bf16[256,1280]{1,0:T(8,128)(2,1)S(1)} %collective-permute-done.slot_ud0) | copy-start | bytes 1966084
  124.3 0.8 copy-start.30
  368.9 1.7 copy-start.24
  368.9 1.7 copy-start.26
  368.9 1.8 copy-start.28
  369.0 26.3 %collective-permute-start.2 = (bf16[256,1920]{1,0:T(8,128)(2,1)S(1)}, bf16[256,1920]{1,0:T(8,128)(2,1)S(1)}, u32[]{:S(2)}, u32[]{:S(2)}) collective-permute-start(bf16[256,1920]{1,0:T(8,128)(2,1)S(1)} %pad_maximum_fusion), channel_id=1, source_target_pairs={{0,0},{1,16},{2,2},{3,18},{4,4},{5,20},{6,6},{7,22},{8,8},{9,24},{... | collective-permute-start | bytes 2949128 | tf_op jit(solution)/shard_map/ppermute | solution.py:327
  370.0 25.3 %collective-permute-start.3 = (bf16[256,1920]{1,0:T(8,128)(2,1)S(1)}, bf16[256,1920]{1,0:T(8,128)(2,1)S(1)}, u32[]{:S(2)}, u32[]{:S(2)}) collective-permute-start(bf16[256,1920]{1,0:T(8,128)(2,1)S(1)} %pad_maximum_fusion.1), channel_id=1, source_target_pairs={{0,8},{1,24},{2,10},{3,26},{4,12},{5,28},{6,14},{7,30},{8,0},{9,16... | collective-permute-start | bytes 2949128 | tf_op jit(solution)/shard_map/ppermute | solution.py:327
  393.5 1.2 copy-start.1
  394.7 0.6 copy-start.19
  534.5 1.0 copy-start.4
  535.6 0.9 copy-start.13
  536.5 0.9 copy-start.14
  537.5 0.9 copy-start.15
  538.4 0.9 copy-start.16
  539.4 3.2 copy-start.31

commit v2 on v1

--- a/solution.py
+++ b/solution.py
@@ -867,7 +867,6 @@
         for n, ref in enumerate((wq_ref, wk_ref, wv_ref)):
             target = held.at[k, :, n * group_width : (n + 1) * group_width]
             way.append(column_go(links, me, k, ref.at[:, cut], target))
-    cot_own, cot_got = gather_rows(1, cot_ref, cot_in)
     for made in small_got:
         made.wait_recv()
     here = small.at[f, :, y]
@@ -884,6 +883,7 @@
     tok_own.wait()
     for made in tok_got:
         made.wait_recv()
+    cot_own, cot_got = gather_rows(1, cot_ref, cot_in)
     wide = [tok_in[i].astype(jnp.float32) for i in range(4)]
     mean = sum(lane_sum(w * w) for w in wide) / (4 * part)
     scale = lax.rsqrt(mean + epsilon)
@@ -892,13 +892,6 @@
         rows_ref[:, here] = tok_in[i]
         normed[0, :, here] = (wide[i] * scale * gain_one[:, here]).astype(jnp.bfloat16)
     first = share_start(links, normed, me)
-    cot_own.wait()
-    for made in cot_got:
-        made.wait_recv()
-    slot = (4 * z + 2 * y + c) * half + lax.broadcasted_iota(jnp.int32, (half, part), 0)
-    valid = slot < jnp.where(x == 0, lengths[0], lengths[1])
-    for i in range(4):
-        grads[:, i * part : (i + 1) * part] = jnp.where(valid, cot_in[i], jnp.zeros_like(cot_in[i]))
     for k in range(2):
         for made in way[3 * k : 3 * k + 3]:
             made.wait_recv()
@@ -945,6 +938,13 @@
                 source = qkv.at[:, 2 * xd + yd, :, here]
                 sent.append(links.go(source, pieces.at[e, :, :, here], device(z, yd, xd, c)))
 
+    cot_own.wait()
+    for made in cot_got:
+        made.wait_recv()
+    slot = (4 * z + 2 * y + c) * half + lax.broadcasted_iota(jnp.int32, (half, part), 0)
+    valid = slot < jnp.where(x == 0, lengths[0], lengths[1])
+    for i in range(4):
+        grads[:, i * part : (i + 1) * part] = jnp.where(valid, cot_in[i], jnp.zeros_like(cot_in[i]))
     order = sum_order(z)
     first[1][0].wait_recv()
     project(0)
@@ -1064,8 +1064,8 @@
 
 def core_kernel(
     ctx_ref, rows_ref, gain_ref, own_ref, slots_o, slots_g, slot_ud0, slot_ud1,
-    residual_ref, context, down, hidden, low, wide_ref, part_ref, pieces, in_gu, in_d,
-    out_weight, gate_up, normed, grads, pre, ctx_all, heads_out, grad_gu, grad_d,
+    layer_ref, context, low, wide_ref, part_ref, pieces, in_gu, in_d,
+    residual_ref, down, hidden, out_weight, gate_up, normed, grads, pre, ctx_all, heads_out, grad_gu, grad_d,
     mine, core_out, core_in, ring_out, ring_in, ring_out2, ring_in2,
     relay_gu, relay_d, send, recv, plane_send, plane_recv, join_send, join_recv, relay_recv,
 ):
@@ -1140,9 +1140,9 @@
     shared = share_start(links, normed, me)
     weight_relay(3)
     share_end(second)
-    for made in state[0]:
+    for made in state[0] + sum(state[1], []):
         links.done(made)
-    ring, terms_go = [], []
+    ring = []
 
     def take_in(i):
         share_step(links, normed, me, shared, i + 1)
@@ -1234,15 +1234,34 @@
 
     shared[1][0].wait_recv()
     context_back(0)
+    for made in (first, following, third, final):
+        links.done(made)
+    layer_core, layer_ring = [], []
+    for i in range(4):
+        terms = right_transposed(pair_rows(hidden, order[i]), down[...])
+        mine[i] = pair_go(links, me, layer_core, i, terms, core_out, core_in)
+
+    def layer_step(i):
+        made = layer_core[i]
+        return sum_step(links, me, made, layer_ring, i, mine[i], core_in, ring_out, ring_in)
+
     for step in (1, 2, 3):
         share_step(links, low, me, shared, step)
         if step == 2:
+            layer_step(0)
             for n, (grad, into, relay) in enumerate(joins):
                 sems = join_send.at[n], join_recv.at[n], relay_recv.at[n]
                 join_relay(links, me, grad, into, relay, *sems)
         for made in shared[1][1 + CHUNKS * (step - 1) : 1 + CHUNKS * step]:
             made.wait_recv()
         context_back(order[step - 1])
+    layer_step(1)
+    layer_step(2)
+    last = layer_step(3)
+    layer = (residual_ref[...] + jnp.concatenate(last, axis=0)).astype(jnp.bfloat16)
+    part = width // 4
+    for i in range(4):
+        layer_ref[i] = layer[:, i * part : (i + 1) * part]
     for made in sent:
         made.wait_recv()
     for n, (_, into, _) in enumerate(joins):
@@ -1270,10 +1289,8 @@
         core_kernel,
         name="core",
         out_shape=[
-            wide_array(rows, width),
+            low_array(4, rows, width // 4),
             low_array(tokens, 4 * size),
-            low_array(8 * depth, ffn),
-            low_array(tokens, ffn),
             low_array(8, rows, width),
             wide_array(rows, width),
             wide_array(1, width),
@@ -1282,8 +1299,11 @@
             low_array(2, 3, depth, ffn),
         ],
         in_specs=[IN_VMEM] * 4 + [IN_PLACE] * 4,
-        out_specs=[IN_VMEM] * 8 + [IN_PLACE] * 2,
+        out_specs=[IN_VMEM] * 6 + [IN_PLACE] * 2,
         scratch_shapes=[
+            pltpu.VMEM((rows, width), jnp.float32),
+            low_space(8 * depth, ffn),
+            low_space(tokens, ffn),
             low_space(8 * depth, group * size),
             low_space(8 * depth, 2 * ffn),
             low_space(8, rows, width),
@@ -1315,12 +1335,12 @@
 
 def exit_kernel(
     piece_ref, normed_ref, weight_ref, token_ref, wide_ref, gain_ref, low_ref, context_ref,
-    hidden_ref, down_ref, residual_ref, gain_two_ref, line_ref, bucket_ref,
+    layer_own, gain_two_ref, line_ref, bucket_ref,
     query_out, key_out, value_out, output_out, home_ref, layer_ref, small_ref,
-    heads_in, rows_low, grad_qkv, grad_out, in_qkv, in_out, held, token_out, layer_own,
+    heads_in, rows_low, weight_grad, weight_in, weight_relay, held, token_out,
     packed, in_f, in_y, in_z,
-    core_out, core_in, ring_out, ring_in, core_out2, core_in2, ring_out2, ring_in2,
-    relay_qkv, relay_out, send, recv, plane_send, plane_recv, relay_recv,
+    core_out, core_in, ring_out, ring_in,
+    send, recv, plane_send, plane_recv, relay_recv,
 ):
     me = z, y, x, c = position()
     greet(*me)
@@ -1328,7 +1348,7 @@
     own, f = 2 * x + y, 2 * x + c
     group, three, size, tokens = heads_in.shape
     rows = tokens // 8
-    depth = grad_qkv.shape[0] // 8
+    depth, cols = weight_grad.shape[1] // 8, weight_grad.shape[2]
     width = normed_ref.shape[2]
     part = width // 4
     heads = []
@@ -1352,60 +1372,35 @@
         into[f] = source[f]
         return got
 
-    ffn, state = ([], []), ([], [])
-    joins = (grad_qkv, in_qkv, relay_qkv), (grad_out, in_out, relay_out)
-
-    def sems(n):
-        return plane_send.at[n], plane_recv.at[n], relay_recv.at[n]
-
-    def ffn_step(i):
-        terms = right_transposed(pair_rows(hidden_ref, order[i]), down_ref[...])
-        return reduce_pair(links, me, ffn, i, terms, core_out2, core_in2, ring_out2, ring_in2)
+    state = [], []
+
+    def join(n):
+        sems = plane_send.at[n], plane_recv.at[n], relay_recv.at[n]
+        return weight_grad.at[n], weight_in.at[n], weight_relay.at[n], *sems
 
     def step(i):
         terms = right_transposed(pair_rows(rows_low, order[i]), weight_ref[...])
         return reduce_pair(links, me, state, i, terms, core_out, core_in, ring_out, ring_in)
 
-    def weight_grads(k, ref, right, join, n):
-        for part_of_rows in range(4):
-            block = 4 * (part_of_rows // 2) + 2 * flip(k, z % 2) + part_of_rows % 2
-            here = pl.ds(pl.multiple_of(block * depth, depth), depth)
-            left = ref[:, :, here].reshape(tokens, depth)
-            join[0][here, :] = left_transposed(left, right[...]).astype(jnp.bfloat16)
-        join_go(links, me, k, *join, *sems(n))
-
-    ffn_step(0)
-    for k in range(2):
-        weight_grads(k, low_ref, context_ref, joins[1], 1)
-    for made in heads:
-        made.wait_recv()
-    for n in range(three):
-        here = slice(n * group * size, (n + 1) * group * size)
-        rows_low[:, here] = heads_in[:, n].reshape(group * size, tokens).T
-    step(0)
-    ffn_step(1)
-    for k in range(2):
-        weight_grads(k, normed_ref, rows_low, joins[0], 0)
-    join_relay(links, me, *joins[1], *sems(1))
-    step(1)
-    ffn_step(2)
-    join_relay(links, me, *joins[0], *sems(0))
-    step(2)
-    last = ffn_step(3)
-    layer = (residual_ref[...] + jnp.concatenate(last, axis=0)).astype(jnp.bfloat16)
-    for i in range(4):
-        layer_own[i] = layer[:, i * part : (i + 1) * part]
-    home = to_home(layer_own, layer_ref)
-    wide_qkv = in_qkv.shape[-1]
-    group_width = wide_qkv // 3
-    cut = pl.ds(pl.multiple_of((z % 2) * group_width, group_width), group_width)
+    def weight_grads(n, ref, right):
+        for k in range(2):
+            for piece in range(4):
+                block = 4 * (piece // 2) + 2 * flip(k, z % 2) + piece % 2
+                here = pl.ds(pl.multiple_of(block * depth, depth), depth)
+                left = ref[:, :, here].reshape(tokens, depth)
+                weight_grad[n, here, :] = left_transposed(left, right).astype(jnp.bfloat16)
+            join_go(links, me, k, *join(n))
+
     way = []
-    for k in range(2):
-        held[k, :, :wide_qkv] = join_sum(k, in_qkv, plane_recv.at[0])
-        held[k, :, wide_qkv:] = join_sum(k, in_out, plane_recv.at[1])
-        for n, ref in enumerate((query_out, key_out, value_out, output_out)):
-            sent = held.at[k, :, n * group_width : (n + 1) * group_width]
-            way.append(column_go(links, me, k, sent, ref.at[:, cut]))
+    results = query_out, key_out, value_out, output_out
+    cut = pl.ds(pl.multiple_of((z % 2) * cols, cols), cols)
+
+    def send_sums(n):
+        for k in range(2):
+            held[n, k] = join_sum(k, weight_in.at[n], plane_recv.at[n])
+            way.append(column_go(links, me, k, held.at[n, k], results[n].at[:, cut]))
+
+    weight_grads(3, low_ref, context_ref[...])
 
     packed[...] = jnp.zeros_like(packed)
     per_block = 4
@@ -1419,6 +1414,24 @@
             value = lane_sum(jnp.where(hot, line_ref[...], 0.0))
             row = jnp.where(lane == n * all_heads + source * (all_heads // 4) + place, value, row)
         packed[block // 2, block % 2, 4:5, :] = row
+    for made in heads:
+        made.wait_recv()
+    for n in range(three):
+        here = slice(n * group * size, (n + 1) * group * size)
+        rows_low[:, here] = heads_in[:, n].reshape(group * size, tokens).T
+    step(0)
+    for n in range(three):
+        weight_grads(n, normed_ref, rows_low[:, n * cols : (n + 1) * cols])
+    join_relay(links, me, *join(3))
+    step(1)
+    send_sums(3)
+    join_relay(links, me, *join(0))
+    join_relay(links, me, *join(1))
+    step(2)
+    join_relay(links, me, *join(2))
+    home = to_home(layer_own, layer_ref)
+    for n in range(three):
+        send_sums(n)
     last = step(3)
     normed_grad = jnp.concatenate(last, axis=0)
     tokens_wide = token_ref[...].astype(jnp.float32)
@@ -1458,7 +1471,7 @@
     links.finish()
 
 
-def leave(pieces, normed, weight, token_rows, wide_grad, gain, low, context, hidden, down, residual,
+def leave(pieces, normed, weight, token_rows, wide_grad, gain, low, context, layer,
           gain_two_part, line_grad, rev_buckets):
     _, _, size, tokens = pieces.shape
     rows, width = token_rows.shape
@@ -1475,36 +1488,31 @@
             low_array(4, rows, width // 4),
             wide_array(*tile),
         ],
-        in_specs=[IN_VMEM] * 14,
+        in_specs=[IN_VMEM] * 12,
         out_specs=[IN_VMEM] * 7,
         scratch_shapes=[
             low_space(4, 3, size, tokens),
             low_space(tokens, wide),
-            low_space(8 * depth, wide),
-            low_space(8 * depth, out_wide),
-            low_space(2, 3, depth, wide),
-            low_space(2, 3, depth, out_wide),
-            low_space(2, depth, wide + out_wide),
-            low_space(4, rows, width // 4),
+            low_space(4, 8 * depth, out_wide),
+            low_space(4, 2, 3, depth, out_wide),
+            low_space(4, 2, depth, out_wide),
+            low_space(4, 2, depth, out_wide),
             low_space(4, rows, width // 4),
             pltpu.VMEM((4, 2, *tile), jnp.float32),
             pltpu.VMEM((3, 4, 2, *tile), jnp.float32),
             pltpu.VMEM((4, *tile), jnp.float32),
             pltpu.VMEM((3, *tile), jnp.float32),
             *reduce_space(rows, width),
-            *reduce_space(rows, width),
-            low_space(2, depth, wide),
-            low_space(2, depth, out_wide),
             COPIES((64,)),
             COPIES((64,)),
-            COPIES((2, 2, 4, 2)),
-            COPIES((2, 2, 3)),
-            COPIES((2, 2)),
+            COPIES((4, 2, 4, 2)),
+            COPIES((4, 2, 3)),
+            COPIES((4, 2)),
         ],
         compiler_params=pltpu.CompilerParams(
             collective_id=4, has_side_effects=True, vmem_limit_bytes=60 << 20
         ),
-    )(pieces, normed, weight, token_rows, wide_grad, gain, low, context, hidden, down, residual,
+    )(pieces, normed, weight, token_rows, wide_grad, gain, low, context, layer,
       gain_two_part, line_grad, rev_buckets)
 
 
@@ -1605,10 +1613,8 @@
     slots_ud = [move(later[k], spread_slot(k)) for k in range(2)]
     context_pieces, context_wide, lse, qkv_all = attend(lengths, pieces, rev_line)
     (
-        residual,
+        layer,
         context,
-        down_full,
-        hidden,
         residual_low,
         residual_grad,
         gain_two_part,
@@ -1638,9 +1644,7 @@
         gain_one,
         residual_low,
         context,
-        hidden,
-        down_full,
-        residual,
+        layer,
         gain_two_part,
         line_grad,
         rev_buckets,

time: 552 us -> 533 us (0.966)
  Pallas kernels: 505 us -> 485 us
    pallas_call x1, Pallas kernels: 136 us -> 117 us  [leave(): pl.pallas_call(exit_kernel, name='leave', out_shape=[*(low_array(depth, c...]
where the time goes in v2:
time: 533 us; the launch traced here: 524 us
  Pallas kernels  485 us (91%)
  local copies, waits for them, and re-layouts  24.6 us (5%)
  other arithmetic  6.23 us (1%)
    pallas_call x1, Pallas kernels, core(): pl.pallas_call(core_kernel, name='core', out_shape=[low_array(4, rows, wi...  238 us
    pallas_call x1, Pallas kernels, leave(): pl.pallas_call(exit_kernel, name='leave', out_shape=[*(low_array(depth, c...  117 us
    pallas_call x1, Pallas kernels, entry(): pl.pallas_call(entry_kernel, name='entry', out_shape=[low_array(rows, wid...  89.3 us
    pallas_call x1, Pallas kernels, attend_back(): pl.pallas_call(attend_back_kernel, name='attend_back', out_shape=[jax.Sha...  22.5 us
    unnamed x71, local copies, waits for them, and re-layouts  19.7 us
    pallas_call x1, Pallas kernels, attend(): pl.pallas_call(attend_kernel, name='attend', out_shape=[jax.ShapeDtypeStr...  15 us
  transfers between devices with their start and end apart: 4, of which 1 were waited for; matrix products, arithmetic and copies ran while one was open for 0% of the time, Pallas kernels for 7%

profile of v2, /device:TPU:0, one launch (start us, length us, event | category | flops | bytes accessed | tf_op | source)
XLA Modules:
  0.0 524.3 jit_solution(9352456835648821524)
XLA Ops:
  0.7 0.8 reshape.43
  1.4 0.8 reverse
  2.2 0.1 slice.35
  2.3 0.1 pad_add_fusion
  2.4 1.4 constant_dynamic-slice_fusion.1
  4.1 0.4 copy-done.32
  4.5 0.1 fusion.small_ref
  4.6 0.4 copy-done.2
  4.9 0.2 copy-done.5
  5.1 0.3 copy-done.6
  5.5 89.3 %entry.1 = (bf16[128,2048]{1,0:T(8,128)(2,1)S(1)}, bf16[8,128,2048]{2,1,0:T(8,128)(2,1)}, bf16[128,2048]{1,0:T(8,128)(2,1)S(1)}, bf16[4,3,64,1024]{3,2,1,0:T(8,1...) custom-call(s32[2]{0:T(128)S(1)} %copy-done.22, ...), custom_call_target="tpu_custom_call" | custom-call | tf_op jit(solution)/shard_map/entry/pallas_call | solution.py:980
  94.8 0.8 copy-done
  95.6 0.8 copy-done.3
  96.4 0.8 copy-done.7
  97.2 0.7 copy-done.17
  97.9 0.6 copy-done.20
  98.5 0.6 copy-done.21
  99.1 0.7 collective-permute-start
  99.9 1.4 copy-done.23
  101.3 15.0 %attend.1 = (bf16[4,64,1024]{2,1,0:T(8,128)(2,1)S(1)}, f32[2,64,2048]{2,1,0:T(8,128)S(1)}, f32[2,1,2048]{2,1,0:T(1,128)S(1)}, bf16[2,3,64,2048]{3,2,1,0:T(8,128)(2,1)S(1)}) custom-call(s32[2]{0:T(128)S(1)} %copy-done.22, bf16[4,3,64,1024]{3,2,1,0:T(8,128)(2,1)S(1)} %copy-done.23, f32[1,4096]{1,0:T(1,128)S(1)} %get-tuple-element.59.rev_ref), custom_call_target="tpu_custom_call" | custom-call | flops 46000001024 | bytes 4194304 | tf_op jit(solution)/shard_map/attend/pallas_call | solution.py:438
  116.3 0.8 copy-done.8
  117.1 1.2 copy-done.25
  118.3 1.0 copy-done.27
  119.2 5.2 %collective-permute-done.1.slot_ud1 = bf16[256,1280]{1,0:T(8,128)(2,1)S(1)} collective-permute-done((bf16[256,1280]{1,0:T(8,128)(2,1)S(1)}, bf16[256,1280]{1,0:T(8,128)(2,1)S(1)}, u32[]{:S(2)}, u32[]{:S(2)}) %collective-permute-start.1) | collective-permute-done | bytes 655392 | tf_op jit(solution)/shard_map/ppermute | solution.py:327
  124.5 0.8 copy-done.30
  125.3 237.9 %core.1 = (bf16[4,128,512]{2,1,0:T(8,128)(2,1)}, bf16[1024,256]{1,0:T(8,128)(2,1)}, bf16[8,128,2048]{2,1,0:T(8,128)(2,1)}, f32[128,2048]{1,0:T(8,128)}, f32[1,20...) custom-call(bf16[4,64,1024]{2,1,0:T(8,128)(2,1)} %copy-done.8, ...), custom_call_target="tpu_custom_call" | custom-call | tf_op jit(solution)/shard_map/core/pallas_call | solution.py:1288
  363.2 2.1 slice_reduce_fusion.2
  365.3 3.7 slice_reduce_fusion
  369.1 0.1 pad_maximum_fusion
  369.2 0.9 collective-permute-start.2
  370.1 0.3 collective-permute-start.3
  370.4 0.3 copy-done.26
  370.6 0.3 copy-done.28
  370.9 22.5 %attend_back.1 = (bf16[4,3,64,1024]{3,2,1,0:T(8,128)(2,1)S(1)}, f32[1,4096]{1,0:T(1,128)S(1)}) custom-call(s32[2]{0:T(128)S(1)} %copy-done.22, bf16[4,64,1024]{2,1,0:T(8,128)(2,1)S(1)} %copy-done.24, f32[1,4096]{1,0:T(1,128)S(1)} %get-tuple-element.59.rev_ref, f32[2,64,2048]{2,1,0:T(8,128)S(1)} %copy-done.28, f32[2,1,2048]{2,1,0:T(1,128)S(1)} %get-tuple-element.70.lse_ref, ...), custom_call_target="tpu_custom_call" | custom-call | flops 46000001024 | bytes 4194304 | tf_op jit(solution)/shard_map/attend_back/pallas_call | solution.py:559
  393.5 1.2 copy-done.1
  394.6 0.6 copy-done.19
  395.2 117.0 %leave.1 = (bf16[256,512]{1,0:T(8,128)(2,1)}, bf16[256,512]{1,0:T(8,128)(2,1)}, bf16[256,512]{1,0:T(8,128)(2,1)}, bf16[256,512]{1,0:T(8,128)(2,1)}, bf16[4,128,5...) custom-call(bf16[4,3,64,1024]{3,2,1,0:T(8,128)(2,1)} %copy-done.1, ...), custom_call_target="tpu_custom_call" | custom-call | tf_op jit(solution)/shard_map/leave/pallas_call | solution.py:1482
  512.3 0.7 slice_reduce_fusion.4
  512.9 1.3 slice_bitcast_fusion
  514.3 0.1 reshape_squeeze.3
  514.4 0.7 constant_dynamic-slice_fusion
  515.0 1.0 copy-done.4
  516.1 0.9 copy-done.13
  517.0 0.9 copy-done.14
  518.0 0.9 copy-done.15
  518.9 0.9 copy-done.16
  519.9 3.2 widen.1
  523.1 0.8 copy.27
  (52 shorter events, 0.5 us)
Async XLA Ops:
  2.4 2.2 copy-start.18
  2.4 2.2 copy-start.12
  3.8 0.7 copy-start.32
  3.8 0.7 copy-start.33
  3.8 1.1 copy-start.2
  3.9 1.2 copy-start.5
  3.9 1.5 copy-start.6
  3.9 1.5 copy-start.9
  3.9 1.5 copy-start.10
  3.9 1.6 copy-start.11
  3.9 1.6 copy-start.22
  94.8 0.8 copy-start
  95.6 0.8 copy-start.3
  96.4 0.8 copy-start.7
  97.2 0.7 copy-start.17
  97.9 0.6 copy-start.20
  98.5 0.6 copy-start.21
  99.1 20.1 %collective-permute-start = (bf16[256,1280]{1,0:T(8,128)(2,1)S(1)}, bf16[256,1280]{1,0:T(8,128)(2,1)S(1)}, u32[]{:S(2)}, u32[]{:S(2)}) collective-permute-start(bf16[256,1280]{1,0:T(8,128)(2,1)S(1)} %pad_maximum_fusion.2), channel_id=1, source_target_pairs={{0,0},{1,16},{2,2},{3,18},{4,4},{5,20},{6,6},{7,22},{8,8},{9,24},{... | collective-permute-start | bytes 1966088 | tf_op jit(solution)/shard_map/ppermute | solution.py:327
  99.8 24.7 %collective-permute-start.1 = (bf16[256,1280]{1,0:T(8,128)(2,1)S(1)}, bf16[256,1280]{1,0:T(8,128)(2,1)S(1)}, u32[]{:S(2)}, u32[]{:S(2)}) collective-permute-start(bf16[256,1280]{1,0:T(8,128)(2,1)S(1)} %pad_maximum_fusion.3), channel_id=1, source_target_pairs={{0,8},{1,24},{2,10},{3,26},{4,12},{5,28},{6,14},{7,30},{8,0},{9,16... | collective-permute-start | bytes 1966088 | tf_op jit(solution)/shard_map/ppermute | solution.py:327
  99.9 1.4 copy-start.23
  116.3 0.8 copy-start.8
  117.1 1.2 copy-start.25
  118.3 1.0 copy-start.27
  119.2 6.1 %copy-start.29 = (bf16[256,1280]{1,0:T(8,128)(2,1)}, bf16[256,1280]{1,0:T(8,128)(2,1)S(1)}, u32[]{:S(2)}) copy-start(bf16[256,1280]{1,0:T(8,128)(2,1)S(1)} %collective-permute-done.slot_ud0) | copy-start | bytes 1966084
  124.5 0.8 copy-start.30
  369.1 1.3 copy-start.24
  369.1 1.6 copy-start.26
  369.1 1.8 copy-start.28
  369.2 26.1 %collective-permute-start.2 = (bf16[256,1920]{1,0:T(8,128)(2,1)S(1)}, bf16[256,1920]{1,0:T(8,128)(2,1)S(1)}, u32[]{:S(2)}, u32[]{:S(2)}) collective-permute-start(bf16[256,1920]{1,0:T(8,128)(2,1)S(1)} %pad_maximum_fusion), channel_id=1, source_target_pairs={{0,0},{1,16},{2,2},{3,18},{4,4},{5,20},{6,6},{7,22},{8,8},{9,24},{... | collective-permute-start | bytes 2949128 | tf_op jit(solution)/shard_map/ppermute | solution.py:327
  370.1 25.1 %collective-permute-start.3 = (bf16[256,1920]{1,0:T(8,128)(2,1)S(1)}, bf16[256,1920]{1,0:T(8,128)(2,1)S(1)}, u32[]{:S(2)}, u32[]{:S(2)}) collective-permute-start(bf16[256,1920]{1,0:T(8,128)(2,1)S(1)} %pad_maximum_fusion.1), channel_id=1, source_target_pairs={{0,8},{1,24},{2,10},{3,26},{4,12},{5,28},{6,14},{7,30},{8,0},{9,16... | collective-permute-start | bytes 2949128 | tf_op jit(solution)/shard_map/ppermute | solution.py:327
  393.4 1.2 copy-start.1
  394.6 0.6 copy-start.19
  515.0 1.0 copy-start.4
  516.1 0.9 copy-start.13
  517.0 0.9 copy-start.14
  518.0 0.9 copy-start.15
  518.9 0.9 copy-start.16
  519.9 3.2 copy-start.31
